TPU v7x, 32 devices: a whole 2x2x4 slice. The times are simulated.
32 devices in a mesh: groups: 2 (over x), tiles: 16 (over z, y, core).
Axes of the slice: x: 2, y: 2, z: 4, core: 2. Of those that a mesh axis runs over, the one named last changes fastest.
Arguments:
- obs_position: float32 [2, 65536], P(None, ('groups', 'tiles')), parts along dimension 1, may hold values from 0 to 24, as said below
- obs_sd: float32 [65536], P(('groups', 'tiles')), parts along dimension 0, may hold values from 0.5 to 2
- obs_var: float32 [65536], P(('groups', 'tiles')), parts along dimension 0, may hold values from 0.5 to 2
- innovations: float32 [8, 65536], P(None, ('groups', 'tiles')), parts along dimension 1, may hold values from -12 to 12
- obs_target: int32 [65536], P(('groups', 'tiles')), parts along dimension 0, may hold values from 0 to 32767, as said below
- pair_table: int32 [32, 4, 2], P(('groups', 'tiles')), parts along dimension 0, may hold values from 0 to 15, as said below
- pair_count: int32 [32], P(('groups', 'tiles')), parts along dimension 0, may hold values from 1 to 4, as said below
Outputs:
- solution_field: float32 [8, 65536], P(None, ('groups', 'tiles')), parts along dimension 1
- residual: float32 [8, 65536], P(None, ('groups', 'tiles')), parts along dimension 1
There are 2 independent parts, one for each index of `groups`. A program takes and returns all parts, laid end to end along the dimension named above; each array names one. Nothing has to cross between parts.
Inputs may be any that keep to these rules, and one draw needn't show every extreme that they name: A permutation; the tile of an observation is obs_target // 2048; of the rows of one device at most 192 go to any one tile, and exactly 192 to some tile. `pair_table`: row d holds (d, d), (d, d + 1), ..., (d, d + pair_count[d] - 1) in its first slots and (d, d) in the others; blocks of pairs that are not listed are zero. `pair_count`: equals 4 on some row. `obs_position`: the first coordinates of tile t lie between bounds of their own that rise with t; the second coordinate lies in 0 to 8.
All inputs are finite; a program needn't handle non-finite values.
Results may differ from a plain program's by a relative error of at most 0.0003.
Values sent between devices are 32-bit elements; how exact they have to be, the bound alone decides.
No kernel may reach another device: no remote copies, remote signals or barrier semaphores. Data moves between devices by JAX's collectives and lax.ppermute only.
A program may use at most 64 MiB of HBM per device.

v0:
```python
import functools

import jax
import jax.numpy as jnp
from jax import lax
from jax.experimental import pallas as pl
from jax.experimental.pallas import tpu as pltpu
from jax.sharding import PartitionSpec as P

f32, bf16, i32 = jnp.float32, jnp.bfloat16, jnp.int32
LANES = 128
FIELDS = 16
BINS = 128
GROUP = 4
UNIT = 8
RING = 4
INNER = 8
OUTER = 18
TRANSPOSED = (((1,), (1,)), ((), ()))
VMEM = pl.BlockSpec(memory_space=pltpu.VMEM)
SMEM = pl.BlockSpec(memory_space=pltpu.SMEM)
HBM = pl.BlockSpec(memory_space=pltpu.HBM)
LIMIT = 40 * 2**20


def iota(shape, axis):
    return lax.broadcasted_iota(i32, shape, axis)


def running_sum_weights():
    shape = (LANES, 2 * LANES)
    row, col = iota(shape, 0), iota(shape, 1)
    return jnp.where((row <= col) | (col >= LANES), 1.0, 0.0).astype(bf16)


def dot(a, b):
    return jnp.dot(a, b, preferred_element_type=f32)


def dot_t(a, b):
    return lax.dot_general(a, b, TRANSPOSED, preferred_element_type=f32)


def invert(places, count):
    chunk_rows, lane_rows, here_rows, low_rows = [], [], [], []
    for chunk, place in enumerate(places):
        high = jnp.right_shift(place, 7)
        here = jnp.where(high == iota((count, LANES), 0), 1.0, 0.0)
        here_rows.append(here.astype(bf16))
        chunk_rows.append((here * float(chunk)).astype(bf16))
        lane_rows.append((here * iota((count, LANES), 1).astype(f32)).astype(bf16))
        low = jnp.bitwise_and(place, LANES - 1)
        low_rows.append(jnp.where(low == iota((LANES, LANES), 0), 1.0, 0.0).astype(bf16))
    left = jnp.concatenate(
        [jnp.concatenate(rows, axis=1) for rows in (chunk_rows, lane_rows, here_rows)], axis=0
    )
    found = dot_t(left, jnp.concatenate(low_rows, axis=1))
    chunk = found[:count].astype(i32)
    lane = found[count : 2 * count].astype(i32)
    return chunk, lane, found[2 * count :] > 0.5


def pick(load, sources, chunk, lane, here):
    total = None
    for source in range(sources):
        value = load(source)
        index = jnp.broadcast_to(lane, value.shape)
        value = jnp.take_along_axis(value, index, axis=1)
        total = value if total is None else jnp.where(chunk == source, value, total)
    return jnp.where(here, total, 0.0)


def outbox_kernel(
    tiles,
    width,
    pos_ref,
    sd_ref,
    var_ref,
    innov_ref,
    target_ref,
    out_ref,
    fields,
    pos_scr,
    sd_scr,
    var_scr,
    innov_scr,
    target_scr,
    inv_chunk,
    inv_lane,
    inv_here,
    sems,
):
    rows = pos_ref.shape[1]
    chunks = rows // LANES
    copies = [
        pltpu.make_async_copy(source, target, sems.at[k])
        for k, (source, target) in enumerate(
            (
                (target_ref, target_scr),
                (pos_ref, pos_scr),
                (sd_ref, sd_scr),
                (var_ref, var_scr),
                (innov_ref, innov_scr),
            )
        )
    ]
    for copy in copies:
        copy.start()
    fields[...] = jnp.zeros_like(fields)
    for copy in copies:
        copy.wait()
    fields[0:2, :] = pos_scr[...]
    fields[2:3, :] = sd_scr[...]
    fields[3:4, :] = var_scr[...]
    target = target_scr[...]
    owner = target // rows
    fields[12:13, :] = (target - owner * rows + 1).astype(f32)
    fields[4:12, :] = innov_scr[...]
    mine = [
        jnp.where(owner[:, c * LANES : (c + 1) * LANES] == iota((tiles, LANES), 0), 1.0, 0.0)
        for c in range(chunks)
    ]
    sums = dot(jnp.concatenate([m.astype(bf16) for m in mine], axis=0), running_sum_weights())
    before = (iota((tiles, LANES), 0) * width - 1).astype(f32)
    places = []
    for c in range(chunks):
        part = sums[c * tiles : (c + 1) * tiles]
        place = jnp.sum(mine[c] * (part[:, :LANES] + before), axis=0, keepdims=True)
        places.append(place.astype(i32))
        before = before + part[:, LANES:]
    count = tiles * width // LANES
    chunk, lane, here = invert(places, count)
    inv_chunk[...] = chunk
    inv_lane[...] = lane
    inv_here[...] = jnp.where(here, 1, 0)
    per_tile = width // LANES
    for d in range(count):
        value = pick(
            lambda s: fields[:, s * LANES : (s + 1) * LANES],
            chunks,
            inv_chunk[d : d + 1, :],
            inv_lane[d : d + 1, :],
            inv_here[d : d + 1, :] > 0,
        )
        first = d % per_tile * FIELDS
        if first + FIELDS <= out_ref.shape[1]:
            out_ref[d // per_tile, first : first + FIELDS, :] = value
        else:
            left = iota((FIELDS // 2, LANES), 1) < LANES // 2
            other = pltpu.roll(value[FIELDS // 2 :], LANES // 2, 1)
            out_ref[d // per_tile, first:, :] = jnp.where(left, value[: FIELDS // 2], other)


def sort_kernel(in_ref, count_ref, share_ref, own_ref, inv_chunk, inv_lane, rank_scr):
    tiles, depth, _ = in_ref.shape
    rows = own_ref.shape[1]
    chunks = rows // LANES
    whole = depth // FIELDS
    half = depth % FIELDS
    sources = tiles * whole + (tiles // 2 if half else 0)

    def load(s):
        if s < tiles * whole:
            first = s % whole * FIELDS
            return in_ref[s // whole, first : first + FIELDS, :]
        pair = 2 * (s - tiles * whole)
        one, two = in_ref[pair, whole * FIELDS :, :], in_ref[pair + 1, whole * FIELDS :, :]
        left = iota((half, LANES), 1) < LANES // 2
        return jnp.concatenate(
            [
                jnp.where(left, one, pltpu.roll(two, LANES // 2, 1)),
                jnp.where(left, pltpu.roll(one, LANES // 2, 1), two),
            ],
            axis=0,
        )

    weights = running_sum_weights()
    before = jnp.full((BINS, LANES), -1.0, f32)
    for s in range(sources):
        data = load(s)
        bins = jnp.clip((data[1:2] * (BINS / 8.0)).astype(i32), 0, BINS - 1)
        bins = jnp.where(data[12:13] > 0.5, bins, -1)
        member = jnp.where(bins == iota((BINS, LANES), 0), 1.0, 0.0)
        part = dot(member.astype(bf16), weights)
        rank_scr[s] = member * (part[:, :LANES] + before)
        before = before + part[:, LANES:]
    totals = before + 1.0
    high = jnp.floor(totals * (1.0 / 64.0))
    low = totals - 64.0 * high
    earlier = jnp.where(iota((BINS, BINS), 1) < iota((BINS, BINS), 0), 1.0, 0.0).astype(bf16)
    base = 64.0 * dot(earlier, high.astype(bf16)) + dot(earlier, low.astype(bf16))
    places = []
    for s in range(sources):
        data = load(s)
        bins = jnp.clip((data[1:2] * (BINS / 8.0)).astype(i32), 0, BINS - 1)
        here = data[12:13] > 0.5
        member = jnp.where(bins == iota((BINS, LANES), 0), base, 0.0)
        place = jnp.sum(member + rank_scr[s], axis=0, keepdims=True).astype(i32)
        places.append(jnp.where(here, place, -1))
    chunk, lane, here = invert(places, chunks)
    inv_chunk[...] = chunk
    inv_lane[...] = lane
    for d in range(chunks):
        own_ref[:, d * LANES : (d + 1) * LANES] = pick(
            load, sources, inv_chunk[d : d + 1, :], inv_lane[d : d + 1, :], inv_lane[d : d + 1, :] >= 0
        )
    share_ref[...] = jnp.zeros_like(share_ref)
    share_ref[0:8, :] = own_ref[4:12, :] * (own_ref[2:3, :] * (1.0 / 256.0))
    share_ref[8:10, :] = own_ref[0:2, :] * 4.0
    stat = jnp.zeros((1, LANES), f32)
    for axis in range(2):
        wide = jnp.concatenate(
            [share_ref[8 + axis : 9 + axis, c * LANES : (c + 1) * LANES] for c in range(chunks)], axis=0
        )
        for which, value in ((0, jnp.min(wide, axis=1, keepdims=True)), (1, jnp.max(wide, axis=1, keepdims=True))):
            lanes = iota((chunks, LANES), 1) - chunks * (2 * axis + which)
            stat = stat + jnp.sum(
                jnp.where(lanes == iota((chunks, LANES), 0), value, 0.0), axis=0, keepdims=True
            )
    stat = jnp.where(iota((1, LANES), 1) == 4 * chunks, count_ref[0].astype(f32), stat)
    share_ref[10:11, 0:LANES] = stat


def make_list(hops, tile_ref, own_share, shares, list_ref):
    chunks = list_ref.shape[0]
    my_tile = tile_ref[0]
    own = own_share[10:11, 0:LANES]
    lane, sub = iota((chunks, LANES), 1), iota((chunks, LANES), 0)
    x_low, x_high, y_low, y_high = [
        jnp.sum(jnp.where(lane == sub + chunks * q, own, 0.0), axis=1, keepdims=True) for q in range(4)
    ]
    own_count = own[:, 4 * chunks : 4 * chunks + 1]
    need = jnp.zeros((chunks, LANES), f32)
    for nb, hop in enumerate(hops):
        other = shares[nb][10:11, 0:LANES]
        at = [pltpu.roll(other, (nb * chunks - q * chunks) % LANES, 1) for q in range(4)]
        gap_x = jnp.maximum(jnp.maximum(at[0] - x_high, x_low - at[1]), 0.0)
        gap_y = jnp.maximum(jnp.maximum(at[2] - y_high, y_low - at[3]), 0.0)
        near = gap_x * gap_x + gap_y * gap_y < 16.001
        count = own_count if hop >= 0 else other[:, 4 * chunks : 4 * chunks + 1]
        listed = (count > abs(hop) + 0.5) & (my_tile + hop >= 0)
        inside = (lane >= nb * chunks) & (lane < (nb + 1) * chunks)
        need = need + jnp.where(near & listed & inside, 1.0, 0.0)
    total = dot(need.astype(bf16), running_sum_weights())
    slot = jnp.where(need > 0.5, total[:, :LANES] - 1.0, -1.0)
    numbers = jnp.broadcast_to(iota((8, LANES), 1).astype(f32), (8, LANES)).astype(bf16)
    for r in range(chunks):
        match = jnp.where(slot[r : r + 1] == iota((LANES, LANES), 0).astype(f32), 1.0, 0.0)
        found = dot_t(numbers, match.astype(bf16))[0:1]
        amount = total[r : r + 1, LANES:]
        row = jnp.where(iota((1, LANES), 1).astype(f32) < amount, found, float(len(hops) * chunks))
        row = jnp.where(iota((1, LANES), 1) == LANES - 1, amount, row)
        list_ref[r : r + 1, :] = row.astype(i32)


def load_where(shares, where_scr):
    chunks = shares[0].shape[1] // LANES
    for nb, share in enumerate(shares):
        for c in range(chunks):
            where_scr[nb * chunks + c] = share[8:16, c * LANES : (c + 1) * LANES]
    where_scr[len(shares) * chunks] = jnp.zeros((8, LANES), f32)


def load_vectors(vectors, vec_scr):
    chunks = vectors[0].shape[1] // LANES
    for nb, vector in enumerate(vectors):
        for c in range(chunks):
            value = vector[0:8, c * LANES : (c + 1) * LANES]
            high = value.astype(bf16)
            low = (value - high.astype(f32)).astype(bf16)
            vec_scr[nb * chunks + c] = jnp.concatenate([high, low], axis=0)
    vec_scr[len(vectors) * chunks] = jnp.zeros((16, LANES), bf16)


def block(x_col, y_col, x_row, y_row):
    dx = x_col - x_row
    dy = y_col - y_row
    square = jnp.maximum(dx * dx + dy * dy, 1e-30)
    distance = square * lax.rsqrt(square)
    inside = jnp.maximum(4.0 - distance, 0.0)
    inside = inside * inside
    corr = inside * inside * (distance + 1.0)
    high = corr.astype(bf16)
    return high, (corr - high.astype(f32)).astype(bf16)


def multiply(total, high, low, vec):
    both = jnp.concatenate([high, low], axis=1)
    return total + dot_t(jnp.concatenate([vec, vec], axis=1), both)


def flatten(list_smem, flat, chunks):
    def chunk_rows(r, number):
        def one(g, number):
            flat[number] = r * LANES + g * GROUP
            return number + 1

        return lax.fori_loop(0, (list_smem[r, LANES - 1] + (GROUP - 1)) // GROUP, one, number)

    number = lax.fori_loop(0, chunks, chunk_rows, 0)
    for k in range(UNIT):
        flat[number + k] = LANES - 2 * GROUP
    return (number + UNIT - 1) // UNIT


def own_columns(own_share, columns):
    for r in range(columns.shape[1]):
        column = own_share[8:16, r * LANES : (r + 1) * LANES].T
        for k in range(2):
            columns[k, r] = jnp.broadcast_to(column[:, k : k + 1], (LANES, LANES))


def ring_slot(stage, unit):
    return stage.at[unit % RING]


def group(list_smem, where_scr, vec_scr, columns, entry, total, keep):
    r, start = entry // LANES, entry % LANES
    x_col, y_col = columns[0, r], columns[1, r]
    for j in range(GROUP):
        c = list_smem[r, start + j]
        high, low = block(x_col, y_col, where_scr[c, 0:1, :], where_scr[c, 1:2, :])
        total = multiply(total, high, low, vec_scr[c])
        keep.append((high, low))
    return total


def add_rows(sums, entry, total):
    r = entry // LANES
    sums[r] = sums[r] + (total[0:8] + total[8:16])


def put_rows(out_ref, sums):
    for r in range(sums.shape[0]):
        out_ref[:, r * LANES : (r + 1) * LANES] = sums[r]


def product(list_smem, flat, where_scr, vec_scr, columns, sums, cache_ref, stage, sems):
    room = cache_ref.shape[0] - 1
    blank = jnp.zeros((16, LANES), f32)
    sums[...] = jnp.zeros_like(sums)
    units = flatten(list_smem, flat, sums.shape[0])

    def save(unit):
        return pltpu.make_async_copy(
            ring_slot(stage, unit), cache_ref.at[jnp.minimum(unit, room)], sems.at[unit % RING]
        )

    def one_unit(unit, _):
        pl.when(unit >= RING)(lambda: save(unit - RING).wait())
        slot = unit % RING
        entries = [flat[unit * UNIT + g] for g in range(UNIT)]
        kept, totals = [], []
        for entry in entries:
            totals.append(group(list_smem, where_scr, vec_scr, columns, entry, blank, kept))
        for k, (high, low) in enumerate(kept):
            stage[slot, 2 * k] = high
            stage[slot, 2 * k + 1] = low
        for entry, total in zip(entries, totals):
            add_rows(sums, entry, total)
        save(unit).start()
        return 0

    lax.fori_loop(0, units, one_unit, 0)
    for k in range(RING):
        last = units - 1 - (units - 1 - k) % RING
        pl.when(units > k)(lambda last=last: save(last).wait())


def product_again(list_smem, flat, where_scr, vec_scr, columns, sums, cache_ref, stage, sems, load):
    room = cache_ref.shape[0] - 1
    blank = jnp.zeros((16, LANES), f32)
    sums[...] = jnp.zeros_like(sums)
    units = flatten(list_smem, flat, sums.shape[0])
    ready = jnp.minimum(units, room)

    def fetch(unit):
        return pltpu.make_async_copy(cache_ref.at[unit], ring_slot(stage, unit), sems.at[unit % RING])

    for k in range(RING):
        pl.when(k < ready)(lambda k=k: fetch(k).start())
    load(units > ready)

    def one_unit(unit, _):
        fetch(unit).wait()
        slot = unit % RING
        entries = [flat[unit * UNIT + g] for g in range(UNIT)]
        totals = []
        for g, entry in enumerate(entries):
            r, start = entry // LANES, entry % LANES
            total = blank
            for j in range(GROUP):
                k = g * GROUP + j
                vec = vec_scr[list_smem[r, start + j]]
                total = multiply(total, stage[slot, 2 * k], stage[slot, 2 * k + 1], vec)
            totals.append(total)
        for entry, total in zip(entries, totals):
            add_rows(sums, entry, total)
        pl.when(unit + RING < ready)(lambda: fetch(unit + RING).start())
        return 0

    lax.fori_loop(0, ready, one_unit, 0)

    def fresh(number, _):
        entry = flat[number]
        add_rows(sums, entry, group(list_smem, where_scr, vec_scr, columns, entry, blank, []))
        return 0

    lax.fori_loop(ready * UNIT, units * UNIT, fresh, 0)


def first_sums(hops, tile_ref, own_share, shares, list_ref, cache_ref, scratch):
    list_smem, sem, flat, where_scr, vec_scr, columns, sums, stage, sems = scratch
    make_list(hops, tile_ref, own_share, shares, list_ref)
    copy = pltpu.make_async_copy(list_ref, list_smem, sem)
    copy.start()
    load_where(shares, where_scr)
    load_vectors(shares, vec_scr)
    own_columns(own_share, columns)
    copy.wait()
    product(list_smem, flat, where_scr, vec_scr, columns, sums, cache_ref, stage, sems)
    return sums


def second_sums(list_smem, own_share, shares, vectors, cache_ref, scratch):
    flat, where_scr, vec_scr, columns, sums, stage, sems = scratch

    def load(needed):
        load_vectors(vectors, vec_scr)

        @pl.when(needed)
        def _():
            load_where(shares, where_scr)
            own_columns(own_share, columns)

    product_again(list_smem, flat, where_scr, vec_scr, columns, sums, cache_ref, stage, sems, load)
    return sums


def first_inner_kernel(tile_ref, own_share, out_ref, list_ref, cache_ref, *scratch):
    put_rows(out_ref, first_sums([0], tile_ref, own_share, [own_share], list_ref, cache_ref, scratch))


def first_outer_kernel(hops, tile_ref, own_ref, inner_ref, own_share, *refs):
    n = len(hops)
    shares = refs[:n]
    image_ref, share_ref, list_ref, cache_ref = refs[n : n + 4]
    put_rows(image_ref, first_sums(hops, tile_ref, own_share, shares, list_ref, cache_ref, refs[n + 4 :]))
    field = own_ref[4:12, :]
    image = own_ref[3:4, :] * field + own_ref[2:3, :] * (inner_ref[...] + image_ref[...])
    image_ref[...] = image
    share_ref[...] = image * (own_ref[2:3, :] * (1.0 / 256.0))


def second_inner_kernel(list_smem, own_share, vector, cache_ref, out_ref, *scratch):
    put_rows(out_ref, second_sums(list_smem, own_share, [own_share], [vector], cache_ref, scratch))


def two_sum(a, b):
    total = a + b
    back = total - a
    return total, (a - (total - back)) + (b - back)


def halves(a):
    scaled = a * 4097.0
    high = scaled - (scaled - a)
    return high, a - high


def two_product(a, b):
    total = a * b
    (a_high, a_low), (b_high, b_low) = halves(a), halves(b)
    error = ((a_high * b_high - total) + a_high * b_low + a_low * b_high) + a_low * b_low
    return total, error


def pair_sum(a, b):
    total, rest = two_sum(a[0], b[0])
    rest = rest + (a[1] + b[1])
    high = total + rest
    return high, rest - (high - total)


def pair_product(a, b):
    total, rest = two_product(a[0], b[0])
    rest = rest + (a[0] * b[1] + a[1] * b[0])
    high = total + rest
    return high, rest - (high - total)


def lane_sums(left, right):
    total = (jnp.zeros((8, LANES), f32), jnp.zeros((8, LANES), f32))
    for c in range(left.shape[1] // LANES):
        lanes = slice(c * LANES, (c + 1) * LANES)
        value, error = two_sum(total[0], left[:, lanes] * right[:, lanes])
        total = (value, total[1] + error)
    shift = LANES // 2
    while shift:
        total = pair_sum(total, tuple(pltpu.roll(part, shift, 1) for part in total))
        shift //= 2
    return total


def second_outer_kernel(n, list_smem, own_ref, image_ref, inner_ref, cache_ref, own_share, *refs):
    shares, vectors, twice_ref, dots_ref = refs[:n], refs[n : 2 * n], refs[2 * n], refs[2 * n + 1]
    put_rows(twice_ref, second_sums(list_smem, own_share, shares, vectors, cache_ref, refs[2 * n + 2 :]))
    image = image_ref[...]
    twice = own_ref[3:4, :] * image + own_ref[2:3, :] * (inner_ref[...] + twice_ref[...])
    twice_ref[...] = twice
    field = own_ref[4:12, :]
    lane = iota((8, LANES), 1)
    dots = jnp.zeros((8, LANES), f32)
    pairs = ((field, field), (field, image), (image, image), (field, twice), (image, twice))
    for k, (left, right) in enumerate(pairs):
        value, rest = lane_sums(left, right)
        dots = jnp.where(lane == 2 * k, value, jnp.where(lane == 2 * k + 1, rest, dots))
    dots_ref[...] = jnp.broadcast_to(dots[None], dots_ref.shape)


def place_kernel(own_ref, image_ref, twice_ref, dots_ref, field_out, residual_out, inv_chunk, inv_lane, data_scr):
    chunks = own_ref.shape[1] // LANES

    def held(t):
        part = dots_ref[t]
        return part, pltpu.roll(part, LANES - 1, 1)

    sums = held(0)
    for t in range(1, dots_ref.shape[0]):
        sums = pair_sum(sums, held(t))
    pp, pq, qq, pz, qz = [tuple(part[:, 2 * k : 2 * k + 1] for part in sums) for k in range(5)]
    alpha = pp[0] / pq[0]
    zero = jnp.zeros_like(alpha)
    first = (alpha, zero)
    minus = (-alpha, zero)
    square = pair_product(first, first)
    norm = pair_sum(pair_sum(pp, pair_product((-2.0 * alpha, zero), pq)), pair_product(square, qq))
    beta = norm[0] / pp[0]
    grown = two_sum(jnp.ones_like(beta), beta)
    power = pair_sum(
        pair_product(grown, pair_sum(pair_product(grown, pq), pair_product(minus, pair_sum(qq, pz)))),
        pair_product(square, qz),
    )
    alpha_next = norm[0] / power[0]
    field, image = own_ref[4:12, :], image_ref[...]
    residual = field - alpha * image
    data_scr[0:8, :] = alpha * field + alpha_next * (residual + beta * field)
    data_scr[8:16, :] = residual - alpha_next * ((image - alpha * twice_ref[...]) + beta * image)
    places = [own_ref[12:13, c * LANES : (c + 1) * LANES].astype(i32) - 1 for c in range(chunks)]
    chunk, lane, _ = invert(places, chunks)
    inv_chunk[...] = chunk
    inv_lane[...] = lane
    for d in range(chunks):
        value = pick(
            lambda s: data_scr[:, s * LANES : (s + 1) * LANES],
            chunks,
            inv_chunk[d : d + 1, :],
            inv_lane[d : d + 1, :],
            inv_lane[d : d + 1, :] >= 0,
        )
        field_out[:, d * LANES : (d + 1) * LANES] = value[0:8]
        residual_out[:, d * LANES : (d + 1) * LANES] = value[8:16]


def call(kernel, outs, ins, scratch=(), limit=LIMIT, cost=None):
    return pl.pallas_call(
        kernel,
        out_shape=[jax.ShapeDtypeStruct(shape, kind) for shape, kind in outs],
        in_specs=ins,
        out_specs=[VMEM if len(shape) < 3 or kind != bf16 else HBM for shape, kind in outs],
        scratch_shapes=list(scratch),
        compiler_params=pltpu.CompilerParams(vmem_limit_bytes=limit),
        cost_estimate=cost,
    )


def cost(parts):
    return pl.CostEstimate(flops=parts * 2 * 10**9, bytes_accessed=parts * 10**7, transcendentals=0)


def around(value, hops, tiles):
    return [lax.ppermute(value, "tiles", [(i, (i - hop) % tiles) for i in range(tiles)]) for hop in hops]


def local(obs_position, obs_sd, obs_var, innovations, obs_target, pair_table, pair_count):
    tiles = lax.axis_size("tiles")
    my_tile = lax.axis_index("tiles").astype(i32)
    rows = obs_sd.shape[0]
    chunks = rows // LANES
    hops = [sign * hop for hop in range(1, pair_table.shape[1]) for sign in (1, -1)]
    n = len(hops)
    capacity = 3 * rows // (2 * tiles)
    width = -(-capacity // LANES) * LANES
    boxes = tiles * width // LANES
    folded = capacity > LANES and 0 < capacity % LANES <= LANES // 2 and tiles % 2 == 0
    depth = width // LANES * FIELDS - (FIELDS // 2 if folded else 0)
    arrivals = tiles * (depth // FIELDS) + (tiles // 2 if folded else 0)

    (outbox,) = call(
        functools.partial(outbox_kernel, tiles, width),
        [((tiles, depth, LANES), f32)],
        [HBM] * 5,
        [
            pltpu.VMEM((FIELDS, rows), f32),
            pltpu.VMEM((2, rows), f32),
            pltpu.VMEM((1, rows), f32),
            pltpu.VMEM((1, rows), f32),
            pltpu.VMEM((8, rows), f32),
            pltpu.VMEM((1, rows), i32),
        ]
        + [pltpu.VMEM((boxes, LANES), i32)] * 3
        + [pltpu.SemaphoreType.DMA((5,))],
        64 * 2**20 - 2**16,
    )(obs_position, obs_sd[None], obs_var[None], innovations, obs_target[None])
    inbox = lax.all_to_all(outbox, "tiles", split_axis=0, concat_axis=0, tiled=True)
    share, own = call(
        sort_kernel,
        [((FIELDS, rows), f32), ((FIELDS, rows), f32)],
        [VMEM, SMEM],
        [pltpu.VMEM((chunks, LANES), i32)] * 2 + [pltpu.VMEM((arrivals, BINS, LANES), f32)],
    )(inbox, pair_count)
    shares = around(share, hops, tiles)
    tile = my_tile[None]

    def operands(held):
        return [
            pltpu.SMEM((held * chunks // GROUP + UNIT,), i32),
            pltpu.VMEM((held + 1, 8, LANES), f32),
            pltpu.VMEM((held + 1, 16, LANES), bf16),
            pltpu.VMEM((2, chunks, LANES, LANES), f32),
            pltpu.VMEM((chunks, 8, LANES), f32),
            pltpu.VMEM((RING, UNIT * 2 * GROUP, LANES, LANES), bf16),
            pltpu.SemaphoreType.DMA((RING,)),
        ]

    def kept(held, most):
        units = min(most, -(-held * chunks // (GROUP * UNIT)))
        return (units + 1, UNIT * 2 * GROUP, LANES, LANES)

    listing = [pltpu.SMEM((chunks, LANES), i32), pltpu.SemaphoreType.DMA]
    field_kind = ((8, rows), f32)
    list_kind = ((chunks, LANES), i32)
    held = n * chunks
    inner, near, near_cache = call(
        first_inner_kernel,
        [field_kind, list_kind, (kept(chunks, INNER), bf16)],
        [SMEM, VMEM],
        listing + operands(chunks),
        cost=cost(1),
    )(tile, share)
    image, image_share, far, far_cache = call(
        functools.partial(first_outer_kernel, hops),
        [field_kind, field_kind, list_kind, (kept(held, OUTER), bf16)],
        [SMEM] + [VMEM] * (n + 3),
        listing + operands(held),
        cost=cost(4),
    )(tile, own, inner, share, *shares)
    vectors = around(image_share, hops, tiles)
    (inner_again,) = call(
        second_inner_kernel,
        [field_kind],
        [SMEM, VMEM, VMEM, HBM],
        operands(chunks),
        cost=cost(1),
    )(near, share, image_share, near_cache)
    twice, dots = call(
        functools.partial(second_outer_kernel, n),
        [field_kind, ((tiles, 8, LANES), f32)],
        [SMEM] + [VMEM] * 3 + [HBM] + [VMEM] * (2 * n + 1),
        operands(held),
        cost=cost(3),
    )(far, own, image, inner_again, far_cache, share, *shares, *vectors)
    dots = lax.all_to_all(dots, "tiles", split_axis=0, concat_axis=0, tiled=True)
    return tuple(
        call(
            place_kernel,
            [field_kind] * 2,
            [VMEM] * 4,
            [pltpu.VMEM((chunks, LANES), i32)] * 2 + [pltpu.VMEM((16, rows), f32)],
        )(own, image, twice, dots)
    )


def solution(mesh):
    both = ("groups", "tiles")
    placed = (P(None, both), P(both), P(both), P(None, both), P(both), P(both, None, None), P(both))
    return jax.shard_map(
        local,
        mesh=mesh,
        in_specs=placed,
        out_specs=(P(None, both), P(None, both)),
        check_vma=False,
    )
```

profile of v0, /device:TPU:0, one launch (start us, length us, event | category | flops | bytes accessed | tf_op | source)
XLA Modules:
  0.0 97.3 jit_solution(1231211288047000111)
XLA Ops:
  0.6 3.9 %shard_map.77 = f32[16,24,128]{2,1,0:T(8,128)} custom-call(f32[2,2048]{1,0:T(2,128)} %pos_ref.1, f32[1,2048]{1,0:T(1,128)} %bitcast.4, f32[1,2048]{1,0:T(1,128)} %bitcast.5, f32[8,2048]{1,0:T(8,128)} %innov_ref.1, s32[1,2048]{1,0:T(1,128)} %bitcast.6), custom_call_target="tpu_custom_call" | custom-call | tf_op jit(solution)/shard_map/pallas_call | solution.py:599
  4.6 7.4 %all-to-all-start = ((f32[16,24,128]{2,1,0:T(8,128)}), f32[16,24,128]{2,1,0:T(8,128)S(1)}, u32[]{:S(2)}, u32[]{:S(2)}) async-start(f32[16,24,128]{2,1,0:T(8,128)} %shard_map.77), calls=%async_computation | async-start | bytes 393216 | tf_op jit(solution)/shard_map/all_to_all | solution.py:615
  12.6 8.3 %all-to-all-done.in_ref = f32[16,24,128]{2,1,0:T(8,128)S(1)} async-done(((f32[16,24,128]{2,1,0:T(8,128)}), f32[16,24,128]{2,1,0:T(8,128)S(1)}, u32[]{:S(2)}, u32[]{:S(2)}) %all-to-all-start) | async-done | bytes 196640 | tf_op jit(solution)/shard_map/all_to_all | solution.py:615
  21.0 2.6 %shard_map.78 = (f32[16,2048]{1,0:T(8,128)S(1)}, f32[16,2048]{1,0:T(8,128)S(1)}) custom-call(f32[16,24,128]{2,1,0:T(8,128)S(1)} %all-to-all-done.in_ref, s32[1]{0:T(128)S(6)} %copy.8.count_ref), custom_call_target="tpu_custom_call" | custom-call | tf_op jit(solution)/shard_map/pallas_call | solution.py:616
  23.6 0.1 collective-permute-start.5
  23.7 3.5 %collective-permute-start.4 = (f32[16,2048]{1,0:T(8,128)S(1)}, f32[16,2048]{1,0:T(8,128)S(1)}, u32[]{:S(2)}, u32[]{:S(2)}) collective-permute-start(f32[16,2048]{1,0:T(8,128)S(1)} %get-tuple-element.14.own_share), channel_id=1, source_target_pairs={{0,13},{1,14},{2,15},{3,0},{4,1},{5,2},{6,3},{7,4},{8,5},{9,6},{10... | collective-permute-start | bytes 393224 | tf_op jit(solution)/shard_map/ppermute | solution.py:582
  27.2 0.0 collective-permute-start.3
  27.2 4.7 %collective-permute-start.2 = (f32[16,2048]{1,0:T(8,128)S(1)}, f32[16,2048]{1,0:T(8,128)S(1)}, u32[]{:S(2)}, u32[]{:S(2)}) collective-permute-start(f32[16,2048]{1,0:T(8,128)S(1)} %get-tuple-element.14.own_share), channel_id=1, source_target_pairs={{0,14},{1,15},{2,0},{3,1},{4,2},{5,3},{6,4},{7,5},{8,6},{9,7},{10,... | collective-permute-start | bytes 393224 | tf_op jit(solution)/shard_map/ppermute | solution.py:582
  31.9 0.1 collective-permute-start.1
  32.0 0.0 collective-permute-done.5.refs_5_
  32.0 4.4 %collective-permute-start = (f32[16,2048]{1,0:T(8,128)S(1)}, f32[16,2048]{1,0:T(8,128)S(1)}, u32[]{:S(2)}, u32[]{:S(2)}) collective-permute-start(f32[16,2048]{1,0:T(8,128)S(1)} %get-tuple-element.14.own_share), channel_id=1, source_target_pairs={{0,15},{1,0},{2,1},{3,2},{4,3},{5,4},{6,5},{7,6},{8,7},{9,8},{10,9... | collective-permute-start | bytes 393224 | tf_op jit(solution)/shard_map/ppermute | solution.py:582
  36.4 8.4 %shard_map.79 = (f32[8,2048]{1,0:T(8,128)S(1)}, s32[16,128]{1,0:T(8,128)S(1)}, bf16[9,64,128,128]{3,2,1,0:T(8,128)(2,1)}) custom-call(s32[1]{0:T(128)} %bitcast.3.tile_ref, f32[16,2048]{1,0:T(8,128)S(1)} %get-tuple-element.14.own_share), custom_call_target="tpu_custom_call" | custom-call | flops 2000000000 | bytes 10000000 | tf_op jit(solution)/shard_map/pallas_call | solution.py:644
  44.8 0.0 collective-permute-done.4.refs_4_
  44.8 0.0 collective-permute-done.3.refs_3_
  44.8 0.0 collective-permute-done.2.refs_2_
  44.8 0.0 collective-permute-done.1.refs_1_
  44.8 0.0 collective-permute-done.refs_0_
  44.9 8.5 %shard_map.80 = (f32[8,2048]{1,0:T(8,128)S(1)}, f32[8,2048]{1,0:T(8,128)S(1)}, s32[16,128]{1,0:T(8,128)S(1)}, bf16[19,64,128,128]{3,2,1,0:T(8,128)(2,1)}) custom-call(s32[1]{0:T(128)} %bitcast.3.tile_ref, f32[16,2048]{1,0:T(8,128)S(1)} %get-tuple-element.13.own_ref, f32[8,2048]{1,0:T(8,128)S(1)} %get-tuple-element.15.inner_ref, ...), custom_call_target="tpu_custom_call" | custom-call | flops 8000000000 | bytes 40000000 | tf_op jit(solution)/shard_map/pallas_call | solution.py:651
  53.4 2.9 %collective-permute-start.11 = (f32[8,2048]{1,0:T(8,128)S(1)}, f32[8,2048]{1,0:T(8,128)S(1)}, u32[]{:S(2)}, u32[]{:S(2)}) collective-permute-start(f32[8,2048]{1,0:T(8,128)S(1)} %get-tuple-element.19.vector), channel_id=1, source_target_pairs={{0,3},{1,4},{2,5},{3,6},{4,7},{5,8},{6,9},{7,10},{8,11},{9,12},{10... | collective-permute-start | bytes 196616 | tf_op jit(solution)/shard_map/ppermute | solution.py:582
  56.3 6.6 %collective-permute-start.10 = (f32[8,2048]{1,0:T(8,128)S(1)}, f32[8,2048]{1,0:T(8,128)S(1)}, u32[]{:S(2)}, u32[]{:S(2)}) collective-permute-start(f32[8,2048]{1,0:T(8,128)S(1)} %get-tuple-element.19.vector), channel_id=1, source_target_pairs={{0,13},{1,14},{2,15},{3,0},{4,1},{5,2},{6,3},{7,4},{8,5},{9,6},{10... | collective-permute-start | bytes 196616 | tf_op jit(solution)/shard_map/ppermute | solution.py:582
  62.9 0.0 collective-permute-start.9
  62.9 4.7 %collective-permute-start.8 = (f32[8,2048]{1,0:T(8,128)S(1)}, f32[8,2048]{1,0:T(8,128)S(1)}, u32[]{:S(2)}, u32[]{:S(2)}) collective-permute-start(f32[8,2048]{1,0:T(8,128)S(1)} %get-tuple-element.19.vector), channel_id=1, source_target_pairs={{0,14},{1,15},{2,0},{3,1},{4,2},{5,3},{6,4},{7,5},{8,6},{9,7},{10,... | collective-permute-start | bytes 196616 | tf_op jit(solution)/shard_map/ppermute | solution.py:582
  67.7 0.0 collective-permute-start.7
  67.7 0.0 collective-permute-done.11.refs_11_
  67.7 4.4 %collective-permute-start.6 = (f32[8,2048]{1,0:T(8,128)S(1)}, f32[8,2048]{1,0:T(8,128)S(1)}, u32[]{:S(2)}, u32[]{:S(2)}) collective-permute-start(f32[8,2048]{1,0:T(8,128)S(1)} %get-tuple-element.19.vector), channel_id=1, source_target_pairs={{0,15},{1,0},{2,1},{3,2},{4,3},{5,4},{6,5},{7,6},{8,7},{9,8},{10,9... | collective-permute-start | bytes 196616 | tf_op jit(solution)/shard_map/ppermute | solution.py:582
  72.1 5.4 %shard_map.81.inner_ref = f32[8,2048]{1,0:T(8,128)S(1)} custom-call(s32[16,128]{1,0:T(8,128)S(1)} %get-tuple-element.18.list_smem, f32[16,2048]{1,0:T(8,128)S(1)} %get-tuple-element.14.own_share, f32[8,2048]{1,0:T(8,128)S(1)} %get-tuple-element.19.vector, bf16[9,64,128,128]{3,2,1,0:T(8,128)(2,1)} %get-tuple-element.20.cache_ref), custom_call_target="tpu_custom_call" | custom-call | flops 2000000000 | bytes 10000000 | tf_op jit(solution)/shard_map/pallas_call | solution.py:659
  77.5 0.0 collective-permute-done.10.refs_10_
  77.6 0.0 collective-permute-done.9.refs_9_
  77.6 0.0 collective-permute-done.8.refs_8_
  77.6 0.0 collective-permute-done.7.refs_7_
  77.6 0.0 collective-permute-done.6.refs_6_
  77.6 6.2 %shard_map.82 = (f32[8,2048]{1,0:T(8,128)S(1)}, f32[16,8,128]{2,1,0:T(8,128)S(1)}) custom-call(s32[16,128]{1,0:T(8,128)S(1)} %get-tuple-element.17.list_smem, f32[16,2048]{1,0:T(8,128)S(1)} %get-tuple-element.13.own_ref, f32[8,2048]{1,0:T(8,128)S(1)} %get-tuple-element.16.image_ref, f32[8,2048]{1,0:T(8,128)S(1)} %shard_map.81.inner_ref, ...), custom_call_target="tpu_custom_call" | custom-call | flops 6000000000 | bytes 30000000 | tf_op jit(solution)/shard_map/pallas_call | solution.py:666
  83.8 11.7 %all_to_all.10.dots_ref = f32[16,8,128]{2,1,0:T(8,128)S(1)} all-to-all(f32[16,8,128]{2,1,0:T(8,128)S(1)} %get-tuple-element.23), channel_id=1, replica_groups=mesh['groups'=2,'tiles'=16] {'tiles'}, dimensions={0} | all-to-all | bytes 131072 | tf_op jit(solution)/shard_map/all_to_all | solution.py:673
  95.4 1.9 %shard_map.83 = (f32[8,2048]{1,0:T(8,128)}, f32[8,2048]{1,0:T(8,128)}) custom-call(f32[16,2048]{1,0:T(8,128)S(1)} %get-tuple-element.13.own_ref, f32[8,2048]{1,0:T(8,128)S(1)} %get-tuple-element.16.image_ref, f32[8,2048]{1,0:T(8,128)S(1)} %get-tuple-element.22.twice_ref, f32[16,8,128]{2,1,0:T(8,128)S(1)} %all_to_all.10.dots_ref), custom_call_target="tpu_custom_call" | custom-call | tf_op jit(solution)/shard_map/pallas_call | solution.py:675
Async XLA Ops:
  4.6 16.4 %all-to-all-start = ((f32[16,24,128]{2,1,0:T(8,128)}), f32[16,24,128]{2,1,0:T(8,128)S(1)}, u32[]{:S(2)}, u32[]{:S(2)}) async-start(f32[16,24,128]{2,1,0:T(8,128)} %shard_map.77), calls=%async_computation | async-start | bytes 393216 | tf_op jit(solution)/shard_map/all_to_all | solution.py:615
  23.6 8.4 %collective-permute-start.5 = (f32[16,2048]{1,0:T(8,128)S(1)}, f32[16,2048]{1,0:T(8,128)S(1)}, u32[]{:S(2)}, u32[]{:S(2)}) collective-permute-start(f32[16,2048]{1,0:T(8,128)S(1)} %get-tuple-element.14.own_share), channel_id=1, source_target_pairs={{0,3},{1,4},{2,5},{3,6},{4,7},{5,8},{6,9},{7,10},{8,11},{9,12},{10... | collective-permute-start | bytes 393224 | tf_op jit(solution)/shard_map/ppermute | solution.py:582
  23.7 21.2 %collective-permute-start.4 = (f32[16,2048]{1,0:T(8,128)S(1)}, f32[16,2048]{1,0:T(8,128)S(1)}, u32[]{:S(2)}, u32[]{:S(2)}) collective-permute-start(f32[16,2048]{1,0:T(8,128)S(1)} %get-tuple-element.14.own_share), channel_id=1, source_target_pairs={{0,13},{1,14},{2,15},{3,0},{4,1},{5,2},{6,3},{7,4},{8,5},{9,6},{10... | collective-permute-start | bytes 393224 | tf_op jit(solution)/shard_map/ppermute | solution.py:582
  27.2 17.6 %collective-permute-start.3 = (f32[16,2048]{1,0:T(8,128)S(1)}, f32[16,2048]{1,0:T(8,128)S(1)}, u32[]{:S(2)}, u32[]{:S(2)}) collective-permute-start(f32[16,2048]{1,0:T(8,128)S(1)} %get-tuple-element.14.own_share), channel_id=1, source_target_pairs={{0,2},{1,3},{2,4},{3,5},{4,6},{5,7},{6,8},{7,9},{8,10},{9,11},{10,... | collective-permute-start | bytes 393224 | tf_op jit(solution)/shard_map/ppermute | solution.py:582
  27.2 17.6 %collective-permute-start.2 = (f32[16,2048]{1,0:T(8,128)S(1)}, f32[16,2048]{1,0:T(8,128)S(1)}, u32[]{:S(2)}, u32[]{:S(2)}) collective-permute-start(f32[16,2048]{1,0:T(8,128)S(1)} %get-tuple-element.14.own_share), channel_id=1, source_target_pairs={{0,14},{1,15},{2,0},{3,1},{4,2},{5,3},{6,4},{7,5},{8,6},{9,7},{10,... | collective-permute-start | bytes 393224 | tf_op jit(solution)/shard_map/ppermute | solution.py:582
  31.9 12.9 %collective-permute-start.1 = (f32[16,2048]{1,0:T(8,128)S(1)}, f32[16,2048]{1,0:T(8,128)S(1)}, u32[]{:S(2)}, u32[]{:S(2)}) collective-permute-start(f32[16,2048]{1,0:T(8,128)S(1)} %get-tuple-element.14.own_share), channel_id=1, source_target_pairs={{0,1},{1,2},{2,3},{3,4},{4,5},{5,6},{6,7},{7,8},{8,9},{9,10},{10,1... | collective-permute-start | bytes 393224 | tf_op jit(solution)/shard_map/ppermute | solution.py:582
  32.0 12.9 %collective-permute-start = (f32[16,2048]{1,0:T(8,128)S(1)}, f32[16,2048]{1,0:T(8,128)S(1)}, u32[]{:S(2)}, u32[]{:S(2)}) collective-permute-start(f32[16,2048]{1,0:T(8,128)S(1)} %get-tuple-element.14.own_share), channel_id=1, source_target_pairs={{0,15},{1,0},{2,1},{3,2},{4,3},{5,4},{6,5},{7,6},{8,7},{9,8},{10,9... | collective-permute-start | bytes 393224 | tf_op jit(solution)/shard_map/ppermute | solution.py:582
  53.4 14.3 %collective-permute-start.11 = (f32[8,2048]{1,0:T(8,128)S(1)}, f32[8,2048]{1,0:T(8,128)S(1)}, u32[]{:S(2)}, u32[]{:S(2)}) collective-permute-start(f32[8,2048]{1,0:T(8,128)S(1)} %get-tuple-element.19.vector), channel_id=1, source_target_pairs={{0,3},{1,4},{2,5},{3,6},{4,7},{5,8},{6,9},{7,10},{8,11},{9,12},{10... | collective-permute-start | bytes 196616 | tf_op jit(solution)/shard_map/ppermute | solution.py:582
  56.3 21.2 %collective-permute-start.10 = (f32[8,2048]{1,0:T(8,128)S(1)}, f32[8,2048]{1,0:T(8,128)S(1)}, u32[]{:S(2)}, u32[]{:S(2)}) collective-permute-start(f32[8,2048]{1,0:T(8,128)S(1)} %get-tuple-element.19.vector), channel_id=1, source_target_pairs={{0,13},{1,14},{2,15},{3,0},{4,1},{5,2},{6,3},{7,4},{8,5},{9,6},{10... | collective-permute-start | bytes 196616 | tf_op jit(solution)/shard_map/ppermute | solution.py:582
  62.9 14.6 %collective-permute-start.9 = (f32[8,2048]{1,0:T(8,128)S(1)}, f32[8,2048]{1,0:T(8,128)S(1)}, u32[]{:S(2)}, u32[]{:S(2)}) collective-permute-start(f32[8,2048]{1,0:T(8,128)S(1)} %get-tuple-element.19.vector), channel_id=1, source_target_pairs={{0,2},{1,3},{2,4},{3,5},{4,6},{5,7},{6,8},{7,9},{8,10},{9,11},{10,... | collective-permute-start | bytes 196616 | tf_op jit(solution)/shard_map/ppermute | solution.py:582
  62.9 14.6 %collective-permute-start.8 = (f32[8,2048]{1,0:T(8,128)S(1)}, f32[8,2048]{1,0:T(8,128)S(1)}, u32[]{:S(2)}, u32[]{:S(2)}) collective-permute-start(f32[8,2048]{1,0:T(8,128)S(1)} %get-tuple-element.19.vector), channel_id=1, source_target_pairs={{0,14},{1,15},{2,0},{3,1},{4,2},{5,3},{6,4},{7,5},{8,6},{9,7},{10,... | collective-permute-start | bytes 196616 | tf_op jit(solution)/shard_map/ppermute | solution.py:582
  67.7 9.9 %collective-permute-start.7 = (f32[8,2048]{1,0:T(8,128)S(1)}, f32[8,2048]{1,0:T(8,128)S(1)}, u32[]{:S(2)}, u32[]{:S(2)}) collective-permute-start(f32[8,2048]{1,0:T(8,128)S(1)} %get-tuple-element.19.vector), channel_id=1, source_target_pairs={{0,1},{1,2},{2,3},{3,4},{4,5},{5,6},{6,7},{7,8},{8,9},{9,10},{10,1... | collective-permute-start | bytes 196616 | tf_op jit(solution)/shard_map/ppermute | solution.py:582
  67.7 9.9 %collective-permute-start.6 = (f32[8,2048]{1,0:T(8,128)S(1)}, f32[8,2048]{1,0:T(8,128)S(1)}, u32[]{:S(2)}, u32[]{:S(2)}) collective-permute-start(f32[8,2048]{1,0:T(8,128)S(1)} %get-tuple-element.19.vector), channel_id=1, source_target_pairs={{0,15},{1,0},{2,1},{3,2},{4,3},{5,4},{6,5},{7,6},{8,7},{9,8},{10,9... | collective-permute-start | bytes 196616 | tf_op jit(solution)/shard_map/ppermute | solution.py:582
where the time goes:
time: 99.3 us; the launch traced here: 97.3 us
  starting transfers between devices  38.9 us (39%)
  Pallas kernels  37 us (37%)
  blocking collectives  11.7 us (12%)
  waiting for transfers between devices  8.38 us (8%)
  between operations  1.43 us (1%)
    ppermute x12, starting transfers between devices, around(): lax.ppermute(value, 'tiles', [(i, (i - hop) % tiles) for i in range(tiles)])  31.5 us
    all_to_all x1, blocking collectives, local(): lax.all_to_all(dots, 'tiles', split_axis=0, concat_axis=0, tiled=True)  11.7 us
    pallas_call x1, Pallas kernels, local(): call(functools.partial(first_outer_kernel, hops), [field_kind, field_kind...  8.52 us
    pallas_call x1, Pallas kernels, local(): call(first_inner_kernel, [field_kind, list_kind, (kept(chunks, INNER), bf...  8.43 us
    all_to_all x1, waiting for transfers between devices, local(): lax.all_to_all(outbox, 'tiles', split_axis=0, concat_axis=0, tiled=True)  8.35 us
    all_to_all x1, starting transfers between devices, local(): lax.all_to_all(outbox, 'tiles', split_axis=0, concat_axis=0, tiled=True)  7.4 us
    pallas_call x1, Pallas kernels, local(): call(functools.partial(second_outer_kernel, n), [field_kind, ((tiles, 8,...  6.17 us
    pallas_call x1, Pallas kernels, local(): call(second_inner_kernel, [field_kind], [SMEM, VMEM, VMEM, HBM], operands...  5.44 us
  transfers between devices with their start and end apart: 13, of which 1 were waited for; matrix products, arithmetic and copies ran while one was open for 0% of the time, Pallas kernels for 14%

commit v1 on v0

--- a/solution.py
+++ b/solution.py
@@ -11,8 +11,9 @@
 LANES = 128
 FIELDS = 16
 BINS = 128
-GROUP = 4
-UNIT = 8
+INNER_GROUP = 2
+OUTER_GROUP = 4
+UNIT = 32
 RING = 4
 INNER = 8
 OUTER = 18
@@ -289,18 +290,19 @@
     return total + dot_t(jnp.concatenate([vec, vec], axis=1), both)
 
 
-def flatten(list_smem, flat, chunks):
+def flatten(size, list_smem, flat, chunks):
     def chunk_rows(r, number):
         def one(g, number):
-            flat[number] = r * LANES + g * GROUP
+            flat[number] = r * LANES + g * size
             return number + 1
 
-        return lax.fori_loop(0, (list_smem[r, LANES - 1] + (GROUP - 1)) // GROUP, one, number)
+        return lax.fori_loop(0, (list_smem[r, LANES - 1] + (size - 1)) // size, one, number)
 
     number = lax.fori_loop(0, chunks, chunk_rows, 0)
-    for k in range(UNIT):
-        flat[number + k] = LANES - 2 * GROUP
-    return (number + UNIT - 1) // UNIT
+    groups = UNIT // size
+    for k in range(groups):
+        flat[number + k] = LANES - 2 * size
+    return (number + groups // 2 - 1) // groups, (number + groups - 1) // groups
 
 
 def own_columns(own_share, columns):
@@ -314,10 +316,10 @@
     return stage.at[unit % RING]
 
 
-def group(list_smem, where_scr, vec_scr, columns, entry, total, keep):
+def group(size, list_smem, where_scr, vec_scr, columns, entry, total, keep):
     r, start = entry // LANES, entry % LANES
     x_col, y_col = columns[0, r], columns[1, r]
-    for j in range(GROUP):
+    for j in range(size):
         c = list_smem[r, start + j]
         high, low = block(x_col, y_col, where_scr[c, 0:1, :], where_scr[c, 1:2, :])
         total = multiply(total, high, low, vec_scr[c])
@@ -335,43 +337,48 @@
         out_ref[:, r * LANES : (r + 1) * LANES] = sums[r]
 
 
-def product(list_smem, flat, where_scr, vec_scr, columns, sums, cache_ref, stage, sems):
+def product(size, list_smem, flat, where_scr, vec_scr, columns, sums, cache_ref, stage, sems):
     room = cache_ref.shape[0] - 1
     blank = jnp.zeros((16, LANES), f32)
     sums[...] = jnp.zeros_like(sums)
-    units = flatten(list_smem, flat, sums.shape[0])
+    whole, units = flatten(size, list_smem, flat, sums.shape[0])
+    groups = UNIT // size
 
     def save(unit):
         return pltpu.make_async_copy(
             ring_slot(stage, unit), cache_ref.at[jnp.minimum(unit, room)], sems.at[unit % RING]
         )
 
-    def one_unit(unit, _):
+    def one_unit(unit, count):
         pl.when(unit >= RING)(lambda: save(unit - RING).wait())
         slot = unit % RING
-        entries = [flat[unit * UNIT + g] for g in range(UNIT)]
+        entries = [flat[unit * groups + g] for g in range(count)]
         kept, totals = [], []
         for entry in entries:
-            totals.append(group(list_smem, where_scr, vec_scr, columns, entry, blank, kept))
+            totals.append(group(size, list_smem, where_scr, vec_scr, columns, entry, blank, kept))
         for k, (high, low) in enumerate(kept):
             stage[slot, 2 * k] = high
             stage[slot, 2 * k + 1] = low
         for entry, total in zip(entries, totals):
             add_rows(sums, entry, total)
         save(unit).start()
+    def loop(unit, _):
+        one_unit(unit, groups)
         return 0
 
-    lax.fori_loop(0, units, one_unit, 0)
+    lax.fori_loop(0, whole, loop, 0)
+    pl.when(units > whole)(lambda: one_unit(whole, groups // 2))
     for k in range(RING):
         last = units - 1 - (units - 1 - k) % RING
         pl.when(units > k)(lambda last=last: save(last).wait())
 
 
-def product_again(list_smem, flat, where_scr, vec_scr, columns, sums, cache_ref, stage, sems, load):
+def product_again(size, list_smem, flat, where_scr, vec_scr, columns, sums, cache_ref, stage, sems, load):
     room = cache_ref.shape[0] - 1
     blank = jnp.zeros((16, LANES), f32)
     sums[...] = jnp.zeros_like(sums)
-    units = flatten(list_smem, flat, sums.shape[0])
+    whole, units = flatten(size, list_smem, flat, sums.shape[0])
+    groups = UNIT // size
     ready = jnp.minimum(units, room)
 
     def fetch(unit):
@@ -381,35 +388,38 @@
         pl.when(k < ready)(lambda k=k: fetch(k).start())
     load(units > ready)
 
-    def one_unit(unit, _):
+    def one_unit(unit, count):
         fetch(unit).wait()
         slot = unit % RING
-        entries = [flat[unit * UNIT + g] for g in range(UNIT)]
+        entries = [flat[unit * groups + g] for g in range(count)]
         totals = []
         for g, entry in enumerate(entries):
             r, start = entry // LANES, entry % LANES
             total = blank
-            for j in range(GROUP):
-                k = g * GROUP + j
+            for j in range(size):
+                k = g * size + j
                 vec = vec_scr[list_smem[r, start + j]]
                 total = multiply(total, stage[slot, 2 * k], stage[slot, 2 * k + 1], vec)
             totals.append(total)
         for entry, total in zip(entries, totals):
             add_rows(sums, entry, total)
         pl.when(unit + RING < ready)(lambda: fetch(unit + RING).start())
+    def loop(unit, _):
+        one_unit(unit, groups)
         return 0
 
-    lax.fori_loop(0, ready, one_unit, 0)
+    lax.fori_loop(0, jnp.minimum(whole, ready), loop, 0)
+    pl.when((units > whole) & (units == ready))(lambda: one_unit(whole, groups // 2))
 
     def fresh(number, _):
         entry = flat[number]
-        add_rows(sums, entry, group(list_smem, where_scr, vec_scr, columns, entry, blank, []))
+        add_rows(sums, entry, group(size, list_smem, where_scr, vec_scr, columns, entry, blank, []))
         return 0
 
-    lax.fori_loop(ready * UNIT, units * UNIT, fresh, 0)
-
-
-def first_sums(hops, tile_ref, own_share, shares, list_ref, cache_ref, scratch):
+    lax.fori_loop(ready * groups, units * groups, fresh, 0)
+
+
+def first_sums(size, hops, tile_ref, own_share, shares, list_ref, cache_ref, scratch):
     list_smem, sem, flat, where_scr, vec_scr, columns, sums, stage, sems = scratch
     make_list(hops, tile_ref, own_share, shares, list_ref)
     copy = pltpu.make_async_copy(list_ref, list_smem, sem)
@@ -418,11 +428,11 @@
     load_vectors(shares, vec_scr)
     own_columns(own_share, columns)
     copy.wait()
-    product(list_smem, flat, where_scr, vec_scr, columns, sums, cache_ref, stage, sems)
+    product(size, list_smem, flat, where_scr, vec_scr, columns, sums, cache_ref, stage, sems)
     return sums
 
 
-def second_sums(list_smem, own_share, shares, vectors, cache_ref, scratch):
+def second_sums(size, list_smem, own_share, shares, vectors, cache_ref, scratch):
     flat, where_scr, vec_scr, columns, sums, stage, sems = scratch
 
     def load(needed):
@@ -433,19 +443,19 @@
             load_where(shares, where_scr)
             own_columns(own_share, columns)
 
-    product_again(list_smem, flat, where_scr, vec_scr, columns, sums, cache_ref, stage, sems, load)
+    product_again(size, list_smem, flat, where_scr, vec_scr, columns, sums, cache_ref, stage, sems, load)
     return sums
 
 
 def first_inner_kernel(tile_ref, own_share, out_ref, list_ref, cache_ref, *scratch):
-    put_rows(out_ref, first_sums([0], tile_ref, own_share, [own_share], list_ref, cache_ref, scratch))
+    put_rows(out_ref, first_sums(INNER_GROUP, [0], tile_ref, own_share, [own_share], list_ref, cache_ref, scratch))
 
 
 def first_outer_kernel(hops, tile_ref, own_ref, inner_ref, own_share, *refs):
     n = len(hops)
     shares = refs[:n]
     image_ref, share_ref, list_ref, cache_ref = refs[n : n + 4]
-    put_rows(image_ref, first_sums(hops, tile_ref, own_share, shares, list_ref, cache_ref, refs[n + 4 :]))
+    put_rows(image_ref, first_sums(OUTER_GROUP, hops, tile_ref, own_share, shares, list_ref, cache_ref, refs[n + 4 :]))
     field = own_ref[4:12, :]
     image = own_ref[3:4, :] * field + own_ref[2:3, :] * (inner_ref[...] + image_ref[...])
     image_ref[...] = image
@@ -453,7 +463,7 @@
 
 
 def second_inner_kernel(list_smem, own_share, vector, cache_ref, out_ref, *scratch):
-    put_rows(out_ref, second_sums(list_smem, own_share, [own_share], [vector], cache_ref, scratch))
+    put_rows(out_ref, second_sums(INNER_GROUP, list_smem, own_share, [own_share], [vector], cache_ref, scratch))
 
 
 def two_sum(a, b):
@@ -504,7 +514,7 @@
 
 def second_outer_kernel(n, list_smem, own_ref, image_ref, inner_ref, cache_ref, own_share, *refs):
     shares, vectors, twice_ref, dots_ref = refs[:n], refs[n : 2 * n], refs[2 * n], refs[2 * n + 1]
-    put_rows(twice_ref, second_sums(list_smem, own_share, shares, vectors, cache_ref, refs[2 * n + 2 :]))
+    put_rows(twice_ref, second_sums(OUTER_GROUP, list_smem, own_share, shares, vectors, cache_ref, refs[2 * n + 2 :]))
     image = image_ref[...]
     twice = own_ref[3:4, :] * image + own_ref[2:3, :] * (inner_ref[...] + twice_ref[...])
     twice_ref[...] = twice
@@ -622,20 +632,20 @@
     shares = around(share, hops, tiles)
     tile = my_tile[None]
 
-    def operands(held):
+    def operands(held, size):
         return [
-            pltpu.SMEM((held * chunks // GROUP + UNIT,), i32),
+            pltpu.SMEM((held * chunks // size + UNIT,), i32),
             pltpu.VMEM((held + 1, 8, LANES), f32),
             pltpu.VMEM((held + 1, 16, LANES), bf16),
             pltpu.VMEM((2, chunks, LANES, LANES), f32),
             pltpu.VMEM((chunks, 8, LANES), f32),
-            pltpu.VMEM((RING, UNIT * 2 * GROUP, LANES, LANES), bf16),
+            pltpu.VMEM((RING, 2 * UNIT, LANES, LANES), bf16),
             pltpu.SemaphoreType.DMA((RING,)),
         ]
 
     def kept(held, most):
-        units = min(most, -(-held * chunks // (GROUP * UNIT)))
-        return (units + 1, UNIT * 2 * GROUP, LANES, LANES)
+        units = min(most, -(-held * chunks // UNIT))
+        return (units + 1, 2 * UNIT, LANES, LANES)
 
     listing = [pltpu.SMEM((chunks, LANES), i32), pltpu.SemaphoreType.DMA]
     field_kind = ((8, rows), f32)
@@ -645,14 +655,14 @@
         first_inner_kernel,
         [field_kind, list_kind, (kept(chunks, INNER), bf16)],
         [SMEM, VMEM],
-        listing + operands(chunks),
+        listing + operands(chunks, INNER_GROUP),
         cost=cost(1),
     )(tile, share)
     image, image_share, far, far_cache = call(
         functools.partial(first_outer_kernel, hops),
         [field_kind, field_kind, list_kind, (kept(held, OUTER), bf16)],
         [SMEM] + [VMEM] * (n + 3),
-        listing + operands(held),
+        listing + operands(held, OUTER_GROUP),
         cost=cost(4),
     )(tile, own, inner, share, *shares)
     vectors = around(image_share, hops, tiles)
@@ -660,14 +670,14 @@
         second_inner_kernel,
         [field_kind],
         [SMEM, VMEM, VMEM, HBM],
-        operands(chunks),
+        operands(chunks, INNER_GROUP),
         cost=cost(1),
     )(near, share, image_share, near_cache)
     twice, dots = call(
         functools.partial(second_outer_kernel, n),
         [field_kind, ((tiles, 8, LANES), f32)],
         [SMEM] + [VMEM] * 3 + [HBM] + [VMEM] * (2 * n + 1),
-        operands(held),
+        operands(held, OUTER_GROUP),
         cost=cost(3),
     )(far, own, image, inner_again, far_cache, share, *shares, *vectors)
     dots = lax.all_to_all(dots, "tiles", split_axis=0, concat_axis=0, tiled=True)

time: 99.3 us -> 96.9 us (0.976); the launches traced: 97.3 us -> 97.5 us
  starting transfers between devices: 38.9 us -> 32.9 us
  blocking collectives: 11.7 us -> 14.9 us
  Pallas kernels: 37 us -> 39.9 us
    ppermute x12, starting transfers between devices: 31.5 us -> 25.5 us  [around(): lax.ppermute(value, 'tiles', [(i, (i - hop) % tiles) for i in range(tiles)])]
    all_to_all x1, blocking collectives: 11.7 us -> 14.9 us  [local(): lax.all_to_all(dots, 'tiles', split_axis=0, concat_axis=0, tiled=True)]
    pallas_call x1, Pallas kernels: 8.52 us -> 10.6 us  [local(): call(functools.partial(first_outer_kernel, hops), [field_kind, field_kind...]
    pallas_call x1, Pallas kernels: 6.17 us -> 7.36 us  [local(): call(functools.partial(second_outer_kernel, n), [field_kind, ((tiles, 8,...]
where the time goes in v1:
time: 96.9 us; the launch traced here: 97.5 us
  Pallas kernels  39.9 us (41%)
  starting transfers between devices  32.9 us (34%)
  blocking collectives  14.9 us (15%)
  waiting for transfers between devices  8.38 us (9%)
  between operations  1.44 us (1%)
    ppermute x12, starting transfers between devices, around(): lax.ppermute(value, 'tiles', [(i, (i - hop) % tiles) for i in range(tiles)])  25.5 us
    all_to_all x1, blocking collectives, local(): lax.all_to_all(dots, 'tiles', split_axis=0, concat_axis=0, tiled=True)  14.9 us
    pallas_call x1, Pallas kernels, local(): call(functools.partial(first_outer_kernel, hops), [field_kind, field_kind...  10.6 us
    all_to_all x1, waiting for transfers between devices, local(): lax.all_to_all(outbox, 'tiles', split_axis=0, concat_axis=0, tiled=True)  8.35 us
    pallas_call x1, Pallas kernels, local(): call(first_inner_kernel, [field_kind, list_kind, (kept(chunks, INNER), bf...  8.07 us
    all_to_all x1, starting transfers between devices, local(): lax.all_to_all(outbox, 'tiles', split_axis=0, concat_axis=0, tiled=True)  7.4 us
    pallas_call x1, Pallas kernels, local(): call(functools.partial(second_outer_kernel, n), [field_kind, ((tiles, 8,...  7.36 us
    pallas_call x1, Pallas kernels, local(): call(second_inner_kernel, [field_kind], [SMEM, VMEM, VMEM, HBM], operands...  5.36 us
  transfers between devices with their start and end apart: 13, of which 1 were waited for; matrix products, arithmetic and copies ran while one was open for 0% of the time, Pallas kernels for 14%

profile of v1, /device:TPU:0, one launch (start us, length us, event | category | flops | bytes accessed | tf_op | source)
XLA Modules:
  0.0 97.5 jit_solution(14674304045977470102)
XLA Ops:
  0.6 3.9 %shard_map.77 = f32[16,24,128]{2,1,0:T(8,128)} custom-call(f32[2,2048]{1,0:T(2,128)} %pos_ref.1, f32[1,2048]{1,0:T(1,128)} %bitcast.4, f32[1,2048]{1,0:T(1,128)} %bitcast.5, f32[8,2048]{1,0:T(8,128)} %innov_ref.1, s32[1,2048]{1,0:T(1,128)} %bitcast.6), custom_call_target="tpu_custom_call" | custom-call | tf_op jit(solution)/shard_map/pallas_call | solution.py:609
  4.6 7.4 %all-to-all-start = ((f32[16,24,128]{2,1,0:T(8,128)}), f32[16,24,128]{2,1,0:T(8,128)S(1)}, u32[]{:S(2)}, u32[]{:S(2)}) async-start(f32[16,24,128]{2,1,0:T(8,128)} %shard_map.77), calls=%async_computation | async-start | bytes 393216 | tf_op jit(solution)/shard_map/all_to_all | solution.py:625
  12.6 8.3 %all-to-all-done.in_ref = f32[16,24,128]{2,1,0:T(8,128)S(1)} async-done(((f32[16,24,128]{2,1,0:T(8,128)}), f32[16,24,128]{2,1,0:T(8,128)S(1)}, u32[]{:S(2)}, u32[]{:S(2)}) %all-to-all-start) | async-done | bytes 196640 | tf_op jit(solution)/shard_map/all_to_all | solution.py:625
  21.0 2.6 %shard_map.78 = (f32[16,2048]{1,0:T(8,128)S(1)}, f32[16,2048]{1,0:T(8,128)S(1)}) custom-call(f32[16,24,128]{2,1,0:T(8,128)S(1)} %all-to-all-done.in_ref, s32[1]{0:T(128)S(6)} %copy.8.count_ref), custom_call_target="tpu_custom_call" | custom-call | tf_op jit(solution)/shard_map/pallas_call | solution.py:626
  23.6 0.1 collective-permute-start.5
  23.7 3.5 %collective-permute-start.4 = (f32[16,2048]{1,0:T(8,128)S(1)}, f32[16,2048]{1,0:T(8,128)S(1)}, u32[]{:S(2)}, u32[]{:S(2)}) collective-permute-start(f32[16,2048]{1,0:T(8,128)S(1)} %get-tuple-element.14.own_share), channel_id=1, source_target_pairs={{0,13},{1,14},{2,15},{3,0},{4,1},{5,2},{6,3},{7,4},{8,5},{9,6},{10... | collective-permute-start | bytes 393224 | tf_op jit(solution)/shard_map/ppermute | solution.py:592
  27.2 0.0 collective-permute-start.3
  27.2 4.7 %collective-permute-start.2 = (f32[16,2048]{1,0:T(8,128)S(1)}, f32[16,2048]{1,0:T(8,128)S(1)}, u32[]{:S(2)}, u32[]{:S(2)}) collective-permute-start(f32[16,2048]{1,0:T(8,128)S(1)} %get-tuple-element.14.own_share), channel_id=1, source_target_pairs={{0,14},{1,15},{2,0},{3,1},{4,2},{5,3},{6,4},{7,5},{8,6},{9,7},{10,... | collective-permute-start | bytes 393224 | tf_op jit(solution)/shard_map/ppermute | solution.py:592
  31.9 0.1 collective-permute-start.1
  32.0 0.0 collective-permute-done.5.refs_5_
  32.0 4.4 %collective-permute-start = (f32[16,2048]{1,0:T(8,128)S(1)}, f32[16,2048]{1,0:T(8,128)S(1)}, u32[]{:S(2)}, u32[]{:S(2)}) collective-permute-start(f32[16,2048]{1,0:T(8,128)S(1)} %get-tuple-element.14.own_share), channel_id=1, source_target_pairs={{0,15},{1,0},{2,1},{3,2},{4,3},{5,4},{6,5},{7,6},{8,7},{9,8},{10,9... | collective-permute-start | bytes 393224 | tf_op jit(solution)/shard_map/ppermute | solution.py:592
  36.4 8.1 %shard_map.79 = (f32[8,2048]{1,0:T(8,128)S(1)}, s32[16,128]{1,0:T(8,128)S(1)}, bf16[9,64,128,128]{3,2,1,0:T(8,128)(2,1)}) custom-call(s32[1]{0:T(128)} %bitcast.3.tile_ref, f32[16,2048]{1,0:T(8,128)S(1)} %get-tuple-element.14.own_share), custom_call_target="tpu_custom_call" | custom-call | flops 2000000000 | bytes 10000000 | tf_op jit(solution)/shard_map/pallas_call | solution.py:654
  44.4 0.0 collective-permute-done.4.refs_4_
  44.5 0.0 collective-permute-done.3.refs_3_
  44.5 0.0 collective-permute-done.2.refs_2_
  44.5 0.0 collective-permute-done.1.refs_1_
  44.5 0.0 collective-permute-done.refs_0_
  44.5 10.6 %shard_map.80 = (f32[8,2048]{1,0:T(8,128)S(1)}, f32[8,2048]{1,0:T(8,128)S(1)}, s32[16,128]{1,0:T(8,128)S(1)}, bf16[19,64,128,128]{3,2,1,0:T(8,128)(2,1)}) custom-call(s32[1]{0:T(128)} %bitcast.3.tile_ref, f32[16,2048]{1,0:T(8,128)S(1)} %get-tuple-element.13.own_ref, f32[8,2048]{1,0:T(8,128)S(1)} %get-tuple-element.15.inner_ref, ...), custom_call_target="tpu_custom_call" | custom-call | flops 8000000000 | bytes 40000000 | tf_op jit(solution)/shard_map/pallas_call | solution.py:661
  55.2 0.1 collective-permute-start.11
  55.2 3.5 %collective-permute-start.10 = (f32[8,2048]{1,0:T(8,128)S(1)}, f32[8,2048]{1,0:T(8,128)S(1)}, u32[]{:S(2)}, u32[]{:S(2)}) collective-permute-start(f32[8,2048]{1,0:T(8,128)S(1)} %get-tuple-element.19.vector), channel_id=1, source_target_pairs={{0,13},{1,14},{2,15},{3,0},{4,1},{5,2},{6,3},{7,4},{8,5},{9,6},{10... | collective-permute-start | bytes 196616 | tf_op jit(solution)/shard_map/ppermute | solution.py:592
  58.7 4.0 %collective-permute-start.9 = (f32[8,2048]{1,0:T(8,128)S(1)}, f32[8,2048]{1,0:T(8,128)S(1)}, u32[]{:S(2)}, u32[]{:S(2)}) collective-permute-start(f32[8,2048]{1,0:T(8,128)S(1)} %get-tuple-element.19.vector), channel_id=1, source_target_pairs={{0,2},{1,3},{2,4},{3,5},{4,6},{5,7},{6,8},{7,9},{8,10},{9,11},{10,... | collective-permute-start | bytes 196616 | tf_op jit(solution)/shard_map/ppermute | solution.py:592
  62.8 0.7 collective-permute-start.8
  63.5 0.0 collective-permute-start.7
  63.5 0.0 collective-permute-done.11.refs_11_
  63.5 4.4 %collective-permute-start.6 = (f32[8,2048]{1,0:T(8,128)S(1)}, f32[8,2048]{1,0:T(8,128)S(1)}, u32[]{:S(2)}, u32[]{:S(2)}) collective-permute-start(f32[8,2048]{1,0:T(8,128)S(1)} %get-tuple-element.19.vector), channel_id=1, source_target_pairs={{0,15},{1,0},{2,1},{3,2},{4,3},{5,4},{6,5},{7,6},{8,7},{9,8},{10,9... | collective-permute-start | bytes 196616 | tf_op jit(solution)/shard_map/ppermute | solution.py:592
  67.9 5.4 %shard_map.81.inner_ref = f32[8,2048]{1,0:T(8,128)S(1)} custom-call(s32[16,128]{1,0:T(8,128)S(1)} %get-tuple-element.18.list_smem, f32[16,2048]{1,0:T(8,128)S(1)} %get-tuple-element.14.own_share, f32[8,2048]{1,0:T(8,128)S(1)} %get-tuple-element.19.vector, bf16[9,64,128,128]{3,2,1,0:T(8,128)(2,1)} %get-tuple-element.20.cache_ref), custom_call_target="tpu_custom_call" | custom-call | flops 2000000000 | bytes 10000000 | tf_op jit(solution)/shard_map/pallas_call | solution.py:669
  73.3 0.0 collective-permute-done.10.refs_10_
  73.3 0.0 collective-permute-done.9.refs_9_
  73.3 0.0 collective-permute-done.8.refs_8_
  73.3 0.0 collective-permute-done.7.refs_7_
  73.3 0.0 collective-permute-done.6.refs_6_
  73.3 7.4 %shard_map.82 = (f32[8,2048]{1,0:T(8,128)S(1)}, f32[16,8,128]{2,1,0:T(8,128)S(1)}) custom-call(s32[16,128]{1,0:T(8,128)S(1)} %get-tuple-element.17.list_smem, f32[16,2048]{1,0:T(8,128)S(1)} %get-tuple-element.13.own_ref, f32[8,2048]{1,0:T(8,128)S(1)} %get-tuple-element.16.image_ref, f32[8,2048]{1,0:T(8,128)S(1)} %shard_map.81.inner_ref, ...), custom_call_target="tpu_custom_call" | custom-call | flops 6000000000 | bytes 30000000 | tf_op jit(solution)/shard_map/pallas_call | solution.py:676
  80.7 14.9 %all_to_all.10.dots_ref = f32[16,8,128]{2,1,0:T(8,128)S(1)} all-to-all(f32[16,8,128]{2,1,0:T(8,128)S(1)} %get-tuple-element.23), channel_id=1, replica_groups=mesh['groups'=2,'tiles'=16] {'tiles'}, dimensions={0} | all-to-all | bytes 131072 | tf_op jit(solution)/shard_map/all_to_all | solution.py:683
  95.6 1.9 %shard_map.83 = (f32[8,2048]{1,0:T(8,128)}, f32[8,2048]{1,0:T(8,128)}) custom-call(f32[16,2048]{1,0:T(8,128)S(1)} %get-tuple-element.13.own_ref, f32[8,2048]{1,0:T(8,128)S(1)} %get-tuple-element.16.image_ref, f32[8,2048]{1,0:T(8,128)S(1)} %get-tuple-element.22.twice_ref, f32[16,8,128]{2,1,0:T(8,128)S(1)} %all_to_all.10.dots_ref), custom_call_target="tpu_custom_call" | custom-call | tf_op jit(solution)/shard_map/pallas_call | solution.py:685
Async XLA Ops:
  4.6 16.4 %all-to-all-start = ((f32[16,24,128]{2,1,0:T(8,128)}), f32[16,24,128]{2,1,0:T(8,128)S(1)}, u32[]{:S(2)}, u32[]{:S(2)}) async-start(f32[16,24,128]{2,1,0:T(8,128)} %shard_map.77), calls=%async_computation | async-start | bytes 393216 | tf_op jit(solution)/shard_map/all_to_all | solution.py:625
  23.6 8.4 %collective-permute-start.5 = (f32[16,2048]{1,0:T(8,128)S(1)}, f32[16,2048]{1,0:T(8,128)S(1)}, u32[]{:S(2)}, u32[]{:S(2)}) collective-permute-start(f32[16,2048]{1,0:T(8,128)S(1)} %get-tuple-element.14.own_share), channel_id=1, source_target_pairs={{0,3},{1,4},{2,5},{3,6},{4,7},{5,8},{6,9},{7,10},{8,11},{9,12},{10... | collective-permute-start | bytes 393224 | tf_op jit(solution)/shard_map/ppermute | solution.py:592
  23.7 20.8 %collective-permute-start.4 = (f32[16,2048]{1,0:T(8,128)S(1)}, f32[16,2048]{1,0:T(8,128)S(1)}, u32[]{:S(2)}, u32[]{:S(2)}) collective-permute-start(f32[16,2048]{1,0:T(8,128)S(1)} %get-tuple-element.14.own_share), channel_id=1, source_target_pairs={{0,13},{1,14},{2,15},{3,0},{4,1},{5,2},{6,3},{7,4},{8,5},{9,6},{10... | collective-permute-start | bytes 393224 | tf_op jit(solution)/shard_map/ppermute | solution.py:592
  27.2 17.3 %collective-permute-start.3 = (f32[16,2048]{1,0:T(8,128)S(1)}, f32[16,2048]{1,0:T(8,128)S(1)}, u32[]{:S(2)}, u32[]{:S(2)}) collective-permute-start(f32[16,2048]{1,0:T(8,128)S(1)} %get-tuple-element.14.own_share), channel_id=1, source_target_pairs={{0,2},{1,3},{2,4},{3,5},{4,6},{5,7},{6,8},{7,9},{8,10},{9,11},{10,... | collective-permute-start | bytes 393224 | tf_op jit(solution)/shard_map/ppermute | solution.py:592
  27.2 17.3 %collective-permute-start.2 = (f32[16,2048]{1,0:T(8,128)S(1)}, f32[16,2048]{1,0:T(8,128)S(1)}, u32[]{:S(2)}, u32[]{:S(2)}) collective-permute-start(f32[16,2048]{1,0:T(8,128)S(1)} %get-tuple-element.14.own_share), channel_id=1, source_target_pairs={{0,14},{1,15},{2,0},{3,1},{4,2},{5,3},{6,4},{7,5},{8,6},{9,7},{10,... | collective-permute-start | bytes 393224 | tf_op jit(solution)/shard_map/ppermute | solution.py:592
  31.9 12.6 %collective-permute-start.1 = (f32[16,2048]{1,0:T(8,128)S(1)}, f32[16,2048]{1,0:T(8,128)S(1)}, u32[]{:S(2)}, u32[]{:S(2)}) collective-permute-start(f32[16,2048]{1,0:T(8,128)S(1)} %get-tuple-element.14.own_share), channel_id=1, source_target_pairs={{0,1},{1,2},{2,3},{3,4},{4,5},{5,6},{6,7},{7,8},{8,9},{9,10},{10,1... | collective-permute-start | bytes 393224 | tf_op jit(solution)/shard_map/ppermute | solution.py:592
  32.0 12.5 %collective-permute-start = (f32[16,2048]{1,0:T(8,128)S(1)}, f32[16,2048]{1,0:T(8,128)S(1)}, u32[]{:S(2)}, u32[]{:S(2)}) collective-permute-start(f32[16,2048]{1,0:T(8,128)S(1)} %get-tuple-element.14.own_share), channel_id=1, source_target_pairs={{0,15},{1,0},{2,1},{3,2},{4,3},{5,4},{6,5},{7,6},{8,7},{9,8},{10,9... | collective-permute-start | bytes 393224 | tf_op jit(solution)/shard_map/ppermute | solution.py:592
  55.2 8.3 %collective-permute-start.11 = (f32[8,2048]{1,0:T(8,128)S(1)}, f32[8,2048]{1,0:T(8,128)S(1)}, u32[]{:S(2)}, u32[]{:S(2)}) collective-permute-start(f32[8,2048]{1,0:T(8,128)S(1)} %get-tuple-element.19.vector), channel_id=1, source_target_pairs={{0,3},{1,4},{2,5},{3,6},{4,7},{5,8},{6,9},{7,10},{8,11},{9,12},{10... | collective-permute-start | bytes 196616 | tf_op jit(solution)/shard_map/ppermute | solution.py:592
  55.2 18.1 %collective-permute-start.10 = (f32[8,2048]{1,0:T(8,128)S(1)}, f32[8,2048]{1,0:T(8,128)S(1)}, u32[]{:S(2)}, u32[]{:S(2)}) collective-permute-start(f32[8,2048]{1,0:T(8,128)S(1)} %get-tuple-element.19.vector), channel_id=1, source_target_pairs={{0,13},{1,14},{2,15},{3,0},{4,1},{5,2},{6,3},{7,4},{8,5},{9,6},{10... | collective-permute-start | bytes 196616 | tf_op jit(solution)/shard_map/ppermute | solution.py:592
  58.7 14.6 %collective-permute-start.9 = (f32[8,2048]{1,0:T(8,128)S(1)}, f32[8,2048]{1,0:T(8,128)S(1)}, u32[]{:S(2)}, u32[]{:S(2)}) collective-permute-start(f32[8,2048]{1,0:T(8,128)S(1)} %get-tuple-element.19.vector), channel_id=1, source_target_pairs={{0,2},{1,3},{2,4},{3,5},{4,6},{5,7},{6,8},{7,9},{8,10},{9,11},{10,... | collective-permute-start | bytes 196616 | tf_op jit(solution)/shard_map/ppermute | solution.py:592
  62.8 10.5 %collective-permute-start.8 = (f32[8,2048]{1,0:T(8,128)S(1)}, f32[8,2048]{1,0:T(8,128)S(1)}, u32[]{:S(2)}, u32[]{:S(2)}) collective-permute-start(f32[8,2048]{1,0:T(8,128)S(1)} %get-tuple-element.19.vector), channel_id=1, source_target_pairs={{0,14},{1,15},{2,0},{3,1},{4,2},{5,3},{6,4},{7,5},{8,6},{9,7},{10,... | collective-permute-start | bytes 196616 | tf_op jit(solution)/shard_map/ppermute | solution.py:592
  63.5 9.8 %collective-permute-start.7 = (f32[8,2048]{1,0:T(8,128)S(1)}, f32[8,2048]{1,0:T(8,128)S(1)}, u32[]{:S(2)}, u32[]{:S(2)}) collective-permute-start(f32[8,2048]{1,0:T(8,128)S(1)} %get-tuple-element.19.vector), channel_id=1, source_target_pairs={{0,1},{1,2},{2,3},{3,4},{4,5},{5,6},{6,7},{7,8},{8,9},{9,10},{10,1... | collective-permute-start | bytes 196616 | tf_op jit(solution)/shard_map/ppermute | solution.py:592
  63.5 9.9 %collective-permute-start.6 = (f32[8,2048]{1,0:T(8,128)S(1)}, f32[8,2048]{1,0:T(8,128)S(1)}, u32[]{:S(2)}, u32[]{:S(2)}) collective-permute-start(f32[8,2048]{1,0:T(8,128)S(1)} %get-tuple-element.19.vector), channel_id=1, source_target_pairs={{0,15},{1,0},{2,1},{3,2},{4,3},{5,4},{6,5},{7,6},{8,7},{9,8},{10,9... | collective-permute-start | bytes 196616 | tf_op jit(solution)/shard_map/ppermute | solution.py:592

commit v2 on v1

--- a/solution.py
+++ b/solution.py
@@ -15,6 +15,7 @@
 OUTER_GROUP = 4
 UNIT = 32
 RING = 4
+SPAN = 16
 INNER = 8
 OUTER = 18
 TRANSPOSED = (((1,), (1,)), ((), ()))
@@ -292,11 +293,15 @@
 
 def flatten(size, list_smem, flat, chunks):
     def chunk_rows(r, number):
-        def one(g, number):
-            flat[number] = r * LANES + g * size
-            return number + 1
-
-        return lax.fori_loop(0, (list_smem[r, LANES - 1] + (size - 1)) // size, one, number)
+        amount = (list_smem[r, LANES - 1] + (size - 1)) // size
+
+        def four(q, _):
+            for g in range(4):
+                flat[number + 4 * q + g] = r * LANES + (4 * q + g) * size
+            return 0
+
+        lax.fori_loop(0, (amount + 3) // 4, four, 0)
+        return number + amount
 
     number = lax.fori_loop(0, chunks, chunk_rows, 0)
     groups = UNIT // size
@@ -525,7 +530,10 @@
     for k, (left, right) in enumerate(pairs):
         value, rest = lane_sums(left, right)
         dots = jnp.where(lane == 2 * k, value, jnp.where(lane == 2 * k + 1, rest, dots))
-    dots_ref[...] = jnp.broadcast_to(dots[None], dots_ref.shape)
+    row = dots[0:1]
+    for r in range(1, 8):
+        row = row + pltpu.roll(dots[r : r + 1], SPAN * r, 1)
+    dots_ref[...] = jnp.broadcast_to(row[None], dots_ref.shape)
 
 
 def place_kernel(own_ref, image_ref, twice_ref, dots_ref, field_out, residual_out, inv_chunk, inv_lane, data_scr):
@@ -538,6 +546,10 @@
     sums = held(0)
     for t in range(1, dots_ref.shape[0]):
         sums = pair_sum(sums, held(t))
+    sums = [
+        jnp.concatenate([part] + [pltpu.roll(part, LANES - SPAN * r, 1) for r in range(1, 8)], axis=0)
+        for part in sums
+    ]
     pp, pq, qq, pz, qz = [tuple(part[:, 2 * k : 2 * k + 1] for part in sums) for k in range(5)]
     alpha = pp[0] / pq[0]
     zero = jnp.zeros_like(alpha)
@@ -675,7 +687,7 @@
     )(near, share, image_share, near_cache)
     twice, dots = call(
         functools.partial(second_outer_kernel, n),
-        [field_kind, ((tiles, 8, LANES), f32)],
+        [field_kind, ((tiles, 1, LANES), f32)],
         [SMEM] + [VMEM] * 3 + [HBM] + [VMEM] * (2 * n + 1),
         operands(held, OUTER_GROUP),
         cost=cost(3),

time: 96.9 us -> 96.6 us (level)
  Pallas kernels: 39.9 us -> 36.6 us
  starting transfers between devices: 32.9 us -> 35.6 us
    ppermute x12, starting transfers between devices: 25.5 us -> 28.2 us  [around(): lax.ppermute(value, 'tiles', [(i, (i - hop) % tiles) for i in range(tiles)])]
    pallas_call x1, Pallas kernels: 10.6 us -> 8.57 us  [local(): call(functools.partial(first_outer_kernel, hops), [field_kind, field_kind...]
    pallas_call x1, Pallas kernels: 7.36 us -> 6.28 us  [local(): call(functools.partial(second_outer_kernel, n), [field_kind, ((tiles, 1,...]
where the time goes in v2:
time: 96.6 us; the launch traced here: 97.5 us
  Pallas kernels  36.6 us (38%)
  starting transfers between devices  35.6 us (37%)
  blocking collectives  15.5 us (16%)
  waiting for transfers between devices  8.38 us (9%)
  between operations  1.43 us (1%)
    ppermute x12, starting transfers between devices, around(): lax.ppermute(value, 'tiles', [(i, (i - hop) % tiles) for i in range(tiles)])  28.2 us
    all_to_all x1, blocking collectives, local(): lax.all_to_all(dots, 'tiles', split_axis=0, concat_axis=0, tiled=True)  15.5 us
    pallas_call x1, Pallas kernels, local(): call(functools.partial(first_outer_kernel, hops), [field_kind, field_kind...  8.57 us
    all_to_all x1, waiting for transfers between devices, local(): lax.all_to_all(outbox, 'tiles', split_axis=0, concat_axis=0, tiled=True)  8.35 us
    pallas_call x1, Pallas kernels, local(): call(first_inner_kernel, [field_kind, list_kind, (kept(chunks, INNER), bf...  7.99 us
    all_to_all x1, starting transfers between devices, local(): lax.all_to_all(outbox, 'tiles', split_axis=0, concat_axis=0, tiled=True)  7.4 us
    pallas_call x1, Pallas kernels, local(): call(functools.partial(second_outer_kernel, n), [field_kind, ((tiles, 1,...  6.28 us
    pallas_call x1, Pallas kernels, local(): call(second_inner_kernel, [field_kind], [SMEM, VMEM, VMEM, HBM], operands...  5.26 us
  transfers between devices with their start and end apart: 13, of which 1 were waited for; matrix products, arithmetic and copies ran while one was open for 0% of the time, Pallas kernels for 14%

profile of v2, /device:TPU:0, one launch (start us, length us, event | category | flops | bytes accessed | tf_op | source)
XLA Modules:
  0.0 97.5 jit_solution(17916450304490367597)
XLA Ops:
  0.6 3.9 %shard_map.77 = f32[16,24,128]{2,1,0:T(8,128)} custom-call(f32[2,2048]{1,0:T(2,128)} %pos_ref.1, f32[1,2048]{1,0:T(1,128)} %bitcast.4, f32[1,2048]{1,0:T(1,128)} %bitcast.5, f32[8,2048]{1,0:T(8,128)} %innov_ref.1, s32[1,2048]{1,0:T(1,128)} %bitcast.6), custom_call_target="tpu_custom_call" | custom-call | tf_op jit(solution)/shard_map/pallas_call | solution.py:621
  4.6 7.4 %all-to-all-start = ((f32[16,24,128]{2,1,0:T(8,128)}), f32[16,24,128]{2,1,0:T(8,128)S(1)}, u32[]{:S(2)}, u32[]{:S(2)}) async-start(f32[16,24,128]{2,1,0:T(8,128)} %shard_map.77), calls=%async_computation | async-start | bytes 393216 | tf_op jit(solution)/shard_map/all_to_all | solution.py:637
  12.6 8.3 %all-to-all-done.in_ref = f32[16,24,128]{2,1,0:T(8,128)S(1)} async-done(((f32[16,24,128]{2,1,0:T(8,128)}), f32[16,24,128]{2,1,0:T(8,128)S(1)}, u32[]{:S(2)}, u32[]{:S(2)}) %all-to-all-start) | async-done | bytes 196640 | tf_op jit(solution)/shard_map/all_to_all | solution.py:637
  21.0 2.6 %shard_map.78 = (f32[16,2048]{1,0:T(8,128)S(1)}, f32[16,2048]{1,0:T(8,128)S(1)}) custom-call(f32[16,24,128]{2,1,0:T(8,128)S(1)} %all-to-all-done.in_ref, s32[1]{0:T(128)S(6)} %copy.8.count_ref), custom_call_target="tpu_custom_call" | custom-call | tf_op jit(solution)/shard_map/pallas_call | solution.py:638
  23.6 0.1 collective-permute-start.5
  23.7 3.5 %collective-permute-start.4 = (f32[16,2048]{1,0:T(8,128)S(1)}, f32[16,2048]{1,0:T(8,128)S(1)}, u32[]{:S(2)}, u32[]{:S(2)}) collective-permute-start(f32[16,2048]{1,0:T(8,128)S(1)} %get-tuple-element.14.own_share), channel_id=1, source_target_pairs={{0,13},{1,14},{2,15},{3,0},{4,1},{5,2},{6,3},{7,4},{8,5},{9,6},{10... | collective-permute-start | bytes 393224 | tf_op jit(solution)/shard_map/ppermute | solution.py:604
  27.2 0.0 collective-permute-start.3
  27.2 4.7 %collective-permute-start.2 = (f32[16,2048]{1,0:T(8,128)S(1)}, f32[16,2048]{1,0:T(8,128)S(1)}, u32[]{:S(2)}, u32[]{:S(2)}) collective-permute-start(f32[16,2048]{1,0:T(8,128)S(1)} %get-tuple-element.14.own_share), channel_id=1, source_target_pairs={{0,14},{1,15},{2,0},{3,1},{4,2},{5,3},{6,4},{7,5},{8,6},{9,7},{10,... | collective-permute-start | bytes 393224 | tf_op jit(solution)/shard_map/ppermute | solution.py:604
  31.9 0.1 collective-permute-start.1
  32.0 0.0 collective-permute-done.5.refs_5_
  32.0 4.4 %collective-permute-start = (f32[16,2048]{1,0:T(8,128)S(1)}, f32[16,2048]{1,0:T(8,128)S(1)}, u32[]{:S(2)}, u32[]{:S(2)}) collective-permute-start(f32[16,2048]{1,0:T(8,128)S(1)} %get-tuple-element.14.own_share), channel_id=1, source_target_pairs={{0,15},{1,0},{2,1},{3,2},{4,3},{5,4},{6,5},{7,6},{8,7},{9,8},{10,9... | collective-permute-start | bytes 393224 | tf_op jit(solution)/shard_map/ppermute | solution.py:604
  36.4 8.0 %shard_map.79 = (f32[8,2048]{1,0:T(8,128)S(1)}, s32[16,128]{1,0:T(8,128)S(1)}, bf16[9,64,128,128]{3,2,1,0:T(8,128)(2,1)}) custom-call(s32[1]{0:T(128)} %bitcast.3.tile_ref, f32[16,2048]{1,0:T(8,128)S(1)} %get-tuple-element.14.own_share), custom_call_target="tpu_custom_call" | custom-call | flops 2000000000 | bytes 10000000 | tf_op jit(solution)/shard_map/pallas_call | solution.py:666
  44.4 0.0 collective-permute-done.4.refs_4_
  44.4 0.0 collective-permute-done.3.refs_3_
  44.4 0.0 collective-permute-done.2.refs_2_
  44.4 0.0 collective-permute-done.1.refs_1_
  44.4 0.0 collective-permute-done.refs_0_
  44.4 8.6 %shard_map.80 = (f32[8,2048]{1,0:T(8,128)S(1)}, f32[8,2048]{1,0:T(8,128)S(1)}, s32[16,128]{1,0:T(8,128)S(1)}, bf16[19,64,128,128]{3,2,1,0:T(8,128)(2,1)}) custom-call(s32[1]{0:T(128)} %bitcast.3.tile_ref, f32[16,2048]{1,0:T(8,128)S(1)} %get-tuple-element.13.own_ref, f32[8,2048]{1,0:T(8,128)S(1)} %get-tuple-element.15.inner_ref, ...), custom_call_target="tpu_custom_call" | custom-call | flops 8000000000 | bytes 40000000 | tf_op jit(solution)/shard_map/pallas_call | solution.py:673
  53.0 3.7 %collective-permute-start.11 = (f32[8,2048]{1,0:T(8,128)S(1)}, f32[8,2048]{1,0:T(8,128)S(1)}, u32[]{:S(2)}, u32[]{:S(2)}) collective-permute-start(f32[8,2048]{1,0:T(8,128)S(1)} %get-tuple-element.19.vector), channel_id=1, source_target_pairs={{0,3},{1,4},{2,5},{3,6},{4,7},{5,8},{6,9},{7,10},{8,11},{9,12},{10... | collective-permute-start | bytes 196616 | tf_op jit(solution)/shard_map/ppermute | solution.py:604
  56.7 0.0 collective-permute-start.10
  56.7 7.3 %collective-permute-start.9 = (f32[8,2048]{1,0:T(8,128)S(1)}, f32[8,2048]{1,0:T(8,128)S(1)}, u32[]{:S(2)}, u32[]{:S(2)}) collective-permute-start(f32[8,2048]{1,0:T(8,128)S(1)} %get-tuple-element.19.vector), channel_id=1, source_target_pairs={{0,2},{1,3},{2,4},{3,5},{4,6},{5,7},{6,8},{7,9},{8,10},{9,11},{10,... | collective-permute-start | bytes 196616 | tf_op jit(solution)/shard_map/ppermute | solution.py:604
  64.0 0.0 collective-permute-start.8
  64.0 3.8 %collective-permute-start.7 = (f32[8,2048]{1,0:T(8,128)S(1)}, f32[8,2048]{1,0:T(8,128)S(1)}, u32[]{:S(2)}, u32[]{:S(2)}) collective-permute-start(f32[8,2048]{1,0:T(8,128)S(1)} %get-tuple-element.19.vector), channel_id=1, source_target_pairs={{0,1},{1,2},{2,3},{3,4},{4,5},{5,6},{6,7},{7,8},{8,9},{9,10},{10,1... | collective-permute-start | bytes 196616 | tf_op jit(solution)/shard_map/ppermute | solution.py:604
  67.8 0.0 collective-permute-done.11.refs_11_
  67.8 0.6 collective-permute-start.6
  68.4 5.3 %shard_map.81.inner_ref = f32[8,2048]{1,0:T(8,128)S(1)} custom-call(s32[16,128]{1,0:T(8,128)S(1)} %get-tuple-element.18.list_smem, f32[16,2048]{1,0:T(8,128)S(1)} %get-tuple-element.14.own_share, f32[8,2048]{1,0:T(8,128)S(1)} %get-tuple-element.19.vector, bf16[9,64,128,128]{3,2,1,0:T(8,128)(2,1)} %get-tuple-element.20.cache_ref), custom_call_target="tpu_custom_call" | custom-call | flops 2000000000 | bytes 10000000 | tf_op jit(solution)/shard_map/pallas_call | solution.py:681
  73.7 0.0 collective-permute-done.10.refs_10_
  73.7 0.0 collective-permute-done.9.refs_9_
  73.7 0.0 collective-permute-done.8.refs_8_
  73.7 0.0 collective-permute-done.7.refs_7_
  73.7 0.0 collective-permute-done.6.refs_6_
  73.7 6.3 %shard_map.82 = (f32[8,2048]{1,0:T(8,128)S(1)}, f32[16,1,128]{2,1,0:T(1,128)S(1)}) custom-call(s32[16,128]{1,0:T(8,128)S(1)} %get-tuple-element.17.list_smem, f32[16,2048]{1,0:T(8,128)S(1)} %get-tuple-element.13.own_ref, f32[8,2048]{1,0:T(8,128)S(1)} %get-tuple-element.16.image_ref, f32[8,2048]{1,0:T(8,128)S(1)} %shard_map.81.inner_ref, ...), custom_call_target="tpu_custom_call" | custom-call | flops 6000000000 | bytes 30000000 | tf_op jit(solution)/shard_map/pallas_call | solution.py:688
  80.0 15.5 %all_to_all.10.dots_ref = f32[16,1,128]{2,1,0:T(1,128)S(1)} all-to-all(f32[16,1,128]{2,1,0:T(1,128)S(1)} %get-tuple-element.23), channel_id=1, replica_groups=mesh['groups'=2,'tiles'=16] {'tiles'}, dimensions={0} | all-to-all | bytes 16384 | tf_op jit(solution)/shard_map/all_to_all | solution.py:695
  95.6 2.0 %shard_map.83 = (f32[8,2048]{1,0:T(8,128)}, f32[8,2048]{1,0:T(8,128)}) custom-call(f32[16,2048]{1,0:T(8,128)S(1)} %get-tuple-element.13.own_ref, f32[8,2048]{1,0:T(8,128)S(1)} %get-tuple-element.16.image_ref, f32[8,2048]{1,0:T(8,128)S(1)} %get-tuple-element.22.twice_ref, f32[16,1,128]{2,1,0:T(1,128)S(1)} %all_to_all.10.dots_ref), custom_call_target="tpu_custom_call" | custom-call | tf_op jit(solution)/shard_map/pallas_call | solution.py:697
Async XLA Ops:
  4.6 16.4 %all-to-all-start = ((f32[16,24,128]{2,1,0:T(8,128)}), f32[16,24,128]{2,1,0:T(8,128)S(1)}, u32[]{:S(2)}, u32[]{:S(2)}) async-start(f32[16,24,128]{2,1,0:T(8,128)} %shard_map.77), calls=%async_computation | async-start | bytes 393216 | tf_op jit(solution)/shard_map/all_to_all | solution.py:637
  23.6 8.4 %collective-permute-start.5 = (f32[16,2048]{1,0:T(8,128)S(1)}, f32[16,2048]{1,0:T(8,128)S(1)}, u32[]{:S(2)}, u32[]{:S(2)}) collective-permute-start(f32[16,2048]{1,0:T(8,128)S(1)} %get-tuple-element.14.own_share), channel_id=1, source_target_pairs={{0,3},{1,4},{2,5},{3,6},{4,7},{5,8},{6,9},{7,10},{8,11},{9,12},{10... | collective-permute-start | bytes 393224 | tf_op jit(solution)/shard_map/ppermute | solution.py:604
  23.7 20.7 %collective-permute-start.4 = (f32[16,2048]{1,0:T(8,128)S(1)}, f32[16,2048]{1,0:T(8,128)S(1)}, u32[]{:S(2)}, u32[]{:S(2)}) collective-permute-start(f32[16,2048]{1,0:T(8,128)S(1)} %get-tuple-element.14.own_share), channel_id=1, source_target_pairs={{0,13},{1,14},{2,15},{3,0},{4,1},{5,2},{6,3},{7,4},{8,5},{9,6},{10... | collective-permute-start | bytes 393224 | tf_op jit(solution)/shard_map/ppermute | solution.py:604
  27.2 17.2 %collective-permute-start.3 = (f32[16,2048]{1,0:T(8,128)S(1)}, f32[16,2048]{1,0:T(8,128)S(1)}, u32[]{:S(2)}, u32[]{:S(2)}) collective-permute-start(f32[16,2048]{1,0:T(8,128)S(1)} %get-tuple-element.14.own_share), channel_id=1, source_target_pairs={{0,2},{1,3},{2,4},{3,5},{4,6},{5,7},{6,8},{7,9},{8,10},{9,11},{10,... | collective-permute-start | bytes 393224 | tf_op jit(solution)/shard_map/ppermute | solution.py:604
  27.2 17.2 %collective-permute-start.2 = (f32[16,2048]{1,0:T(8,128)S(1)}, f32[16,2048]{1,0:T(8,128)S(1)}, u32[]{:S(2)}, u32[]{:S(2)}) collective-permute-start(f32[16,2048]{1,0:T(8,128)S(1)} %get-tuple-element.14.own_share), channel_id=1, source_target_pairs={{0,14},{1,15},{2,0},{3,1},{4,2},{5,3},{6,4},{7,5},{8,6},{9,7},{10,... | collective-permute-start | bytes 393224 | tf_op jit(solution)/shard_map/ppermute | solution.py:604
  31.9 12.5 %collective-permute-start.1 = (f32[16,2048]{1,0:T(8,128)S(1)}, f32[16,2048]{1,0:T(8,128)S(1)}, u32[]{:S(2)}, u32[]{:S(2)}) collective-permute-start(f32[16,2048]{1,0:T(8,128)S(1)} %get-tuple-element.14.own_share), channel_id=1, source_target_pairs={{0,1},{1,2},{2,3},{3,4},{4,5},{5,6},{6,7},{7,8},{8,9},{9,10},{10,1... | collective-permute-start | bytes 393224 | tf_op jit(solution)/shard_map/ppermute | solution.py:604
  32.0 12.4 %collective-permute-start = (f32[16,2048]{1,0:T(8,128)S(1)}, f32[16,2048]{1,0:T(8,128)S(1)}, u32[]{:S(2)}, u32[]{:S(2)}) collective-permute-start(f32[16,2048]{1,0:T(8,128)S(1)} %get-tuple-element.14.own_share), channel_id=1, source_target_pairs={{0,15},{1,0},{2,1},{3,2},{4,3},{5,4},{6,5},{7,6},{8,7},{9,8},{10,9... | collective-permute-start | bytes 393224 | tf_op jit(solution)/shard_map/ppermute | solution.py:604
  53.0 14.8 %collective-permute-start.11 = (f32[8,2048]{1,0:T(8,128)S(1)}, f32[8,2048]{1,0:T(8,128)S(1)}, u32[]{:S(2)}, u32[]{:S(2)}) collective-permute-start(f32[8,2048]{1,0:T(8,128)S(1)} %get-tuple-element.19.vector), channel_id=1, source_target_pairs={{0,3},{1,4},{2,5},{3,6},{4,7},{5,8},{6,9},{7,10},{8,11},{9,12},{10... | collective-permute-start | bytes 196616 | tf_op jit(solution)/shard_map/ppermute | solution.py:604
  56.7 17.0 %collective-permute-start.10 = (f32[8,2048]{1,0:T(8,128)S(1)}, f32[8,2048]{1,0:T(8,128)S(1)}, u32[]{:S(2)}, u32[]{:S(2)}) collective-permute-start(f32[8,2048]{1,0:T(8,128)S(1)} %get-tuple-element.19.vector), channel_id=1, source_target_pairs={{0,13},{1,14},{2,15},{3,0},{4,1},{5,2},{6,3},{7,4},{8,5},{9,6},{10... | collective-permute-start | bytes 196616 | tf_op jit(solution)/shard_map/ppermute | solution.py:604
  56.7 17.0 %collective-permute-start.9 = (f32[8,2048]{1,0:T(8,128)S(1)}, f32[8,2048]{1,0:T(8,128)S(1)}, u32[]{:S(2)}, u32[]{:S(2)}) collective-permute-start(f32[8,2048]{1,0:T(8,128)S(1)} %get-tuple-element.19.vector), channel_id=1, source_target_pairs={{0,2},{1,3},{2,4},{3,5},{4,6},{5,7},{6,8},{7,9},{8,10},{9,11},{10,... | collective-permute-start | bytes 196616 | tf_op jit(solution)/shard_map/ppermute | solution.py:604
  64.0 9.7 %collective-permute-start.8 = (f32[8,2048]{1,0:T(8,128)S(1)}, f32[8,2048]{1,0:T(8,128)S(1)}, u32[]{:S(2)}, u32[]{:S(2)}) collective-permute-start(f32[8,2048]{1,0:T(8,128)S(1)} %get-tuple-element.19.vector), channel_id=1, source_target_pairs={{0,14},{1,15},{2,0},{3,1},{4,2},{5,3},{6,4},{7,5},{8,6},{9,7},{10,... | collective-permute-start | bytes 196616 | tf_op jit(solution)/shard_map/ppermute | solution.py:604
  64.0 9.8 %collective-permute-start.7 = (f32[8,2048]{1,0:T(8,128)S(1)}, f32[8,2048]{1,0:T(8,128)S(1)}, u32[]{:S(2)}, u32[]{:S(2)}) collective-permute-start(f32[8,2048]{1,0:T(8,128)S(1)} %get-tuple-element.19.vector), channel_id=1, source_target_pairs={{0,1},{1,2},{2,3},{3,4},{4,5},{5,6},{6,7},{7,8},{8,9},{9,10},{10,1... | collective-permute-start | bytes 196616 | tf_op jit(solution)/shard_map/ppermute | solution.py:604
  67.8 5.9 %collective-permute-start.6 = (f32[8,2048]{1,0:T(8,128)S(1)}, f32[8,2048]{1,0:T(8,128)S(1)}, u32[]{:S(2)}, u32[]{:S(2)}) collective-permute-start(f32[8,2048]{1,0:T(8,128)S(1)} %get-tuple-element.19.vector), channel_id=1, source_target_pairs={{0,15},{1,0},{2,1},{3,2},{4,3},{5,4},{6,5},{7,6},{8,7},{9,8},{10,9... | collective-permute-start | bytes 196616 | tf_op jit(solution)/shard_map/ppermute | solution.py:604
